TPU v7x, 32 devices: a whole 2x2x4 slice. The times are simulated.
32 devices in a mesh: grp: 4 (over z), dp: 8 (over y, x, core).
Axes of the slice: x: 2, y: 2, z: 4, core: 2. Of those that a mesh axis runs over, the one named last changes fastest.
Arguments:
- tokens: bfloat16 [32, 1024, 768], P(('grp', 'dp')), may hold values from -6 to 6
- grad_out: bfloat16 [32, 1024, 768], P(('grp', 'dp')), may hold values from -6 to 6
- lengths: int32 [32], P(('grp', 'dp')), may hold values from 32 to 1024, as said below
- task_of: int32 [32], P(('grp', 'dp')), may hold values from 0 to 15
- task_tokens: int32 [16], replicated, may hold values from 256 to 4096
- w_qkv: bfloat16 [768, 2304], P('dp'), may hold values from -0.21875 to 0.21875
- w_out: bfloat16 [768, 768], P('dp'), may hold values from -1.75 to 1.75
- w_up: bfloat16 [768, 3072], P('dp'), may hold values from -0.21875 to 0.21875
- w_down: bfloat16 [3072, 768], P('dp'), may hold values from -0.109375 to 0.109375
- bias_q: bfloat16 [768], P('dp'), may hold values from -3 to 3
- bias_v: bfloat16 [768], P('dp'), may hold values from -3 to 3
- bias_out: bfloat16 [768], P('dp'), may hold values from -3 to 3
- bias_up: bfloat16 [3072], P('dp'), may hold values from -3 to 3
- bias_down: bfloat16 [768], P('dp'), may hold values from -3 to 3
- gain_one: bfloat16 [768], P('dp'), may hold values from 0.5 to 1.5
- shift_one: bfloat16 [768], P('dp'), may hold values from -3 to 3
- gain_two: bfloat16 [768], P('dp'), may hold values from 0.5 to 1.5
- shift_two: bfloat16 [768], P('dp'), may hold values from -3 to 3
Outputs:
- activations: bfloat16 [32, 1024, 768], P(('grp', 'dp'))
- input_grad: bfloat16 [32, 1024, 768], P(('grp', 'dp'))
- grad_w_qkv: float32 [768, 2304], P('dp')
- grad_w_out: float32 [768, 768], P('dp')
- grad_w_up: float32 [768, 3072], P('dp')
- grad_w_down: float32 [3072, 768], P('dp')
- grad_bias_q: float32 [768], P('dp')
- grad_bias_v: float32 [768], P('dp')
- grad_bias_out: float32 [768], P('dp')
- grad_bias_up: float32 [3072], P('dp')
- grad_bias_down: float32 [768], P('dp')
- grad_gain_one: float32 [768], P('dp')
- grad_shift_one: float32 [768], P('dp')
- grad_gain_two: float32 [768], P('dp')
- grad_shift_two: float32 [768], P('dp')
Inputs may be any that keep to these rules, and one draw needn't show every extreme that they name: `lengths`: every sequence has at least 32 live tokens and at least one has 1024.
All inputs are finite; a program needn't handle non-finite values.
Results may differ from a plain program's by a relative error of at most 0.018.
Values may be sent and summed in bfloat16 or wider, within the bound.
A program may use at most 192 MiB of HBM per device.

v0:
```python
import math

import jax
import jax.numpy as jnp
from jax import lax
from jax.sharding import PartitionSpec as P

HEAD_DIM = 64


EPS = 1e-05
UNIT = 1024.0


def shortened(value):
    return jax.tree.map(lambda a: a.astype(jnp.bfloat16) if a.dtype == jnp.float32 else a, value)


def norm_rows(values):
    mean = jnp.mean(values, axis=-1, keepdims=True)
    centered = values - mean
    rstd = lax.rsqrt(jnp.mean(centered * centered, axis=-1, keepdims=True) + EPS)
    return (centered * rstd, rstd)


def norm_back(grad_norm, normed, rstd):
    mean_one = jnp.mean(grad_norm, axis=-1, keepdims=True)
    mean_two = jnp.mean(grad_norm * normed, axis=-1, keepdims=True)
    return rstd * (grad_norm - mean_one - normed * mean_two)


def gelu_value(values):
    return values * 0.5 * (1.0 + lax.erf(values * (1.0 / math.sqrt(2.0))))


def gelu_slope(values):
    cdf = 0.5 * (1.0 + lax.erf(values * (1.0 / math.sqrt(2.0))))
    dens = jnp.exp(-0.5 * values * values) * (1.0 / math.sqrt(2.0 * math.pi))
    return cdf + values * dens


def left_dot(left, right):
    return lax.dot_general(
        left, right, (((0,), (0,)), ((), ())), preferred_element_type=jnp.float32
    )


def right_dot(left, right):
    return lax.dot_general(
        left, right, (((1,), (1,)), ((), ())), preferred_element_type=jnp.float32
    )


def masked_scores(q_rows, keys, start, length_s, scale):
    block = q_rows.shape[0]
    scores = jnp.einsum("qhd,khd->hqk", q_rows, keys, preferred_element_type=jnp.float32) * scale
    rows = start + jnp.arange(block)
    columns = jnp.arange(keys.shape[0])
    allowed = (columns[None, :] <= rows[:, None]) & (columns[None, :] < length_s)
    return jnp.where(allowed[None], scores, -1e30)


def group_forward(q_group, k_group, v_group, length_s):
    length, width = q_group.shape
    heads_item = width // HEAD_DIM
    block = min(512, length)
    scale = HEAD_DIM ** (-0.5)
    queries = q_group.reshape(length, heads_item, HEAD_DIM)
    keys = k_group.reshape(length, heads_item, HEAD_DIM)
    values = v_group.reshape(length, heads_item, HEAD_DIM)
    pieces = []
    sums = []
    for start in range(0, length, block):
        scores = masked_scores(queries[start : start + block], keys, start, length_s, scale)
        top = jnp.max(scores, axis=-1, keepdims=True)
        lse = top + jnp.log(jnp.sum(jnp.exp(scores - top), axis=-1, keepdims=True))
        probs = jnp.exp(scores - lse).astype(jnp.bfloat16)
        result = jnp.einsum("hqk,khd->qhd", probs, values, preferred_element_type=jnp.float32)
        pieces.append(result.reshape(block, width))
        sums.append(lse)
    return (jnp.concatenate(pieces, axis=0), jnp.concatenate(sums, axis=1))


def group_backward(q_group, k_group, v_group, lse, grad_group, length_s):
    length, width = q_group.shape
    heads_item = width // HEAD_DIM
    block = min(512, length)
    scale = HEAD_DIM ** (-0.5)
    queries = q_group.reshape(length, heads_item, HEAD_DIM)
    keys = k_group.reshape(length, heads_item, HEAD_DIM)
    values = v_group.reshape(length, heads_item, HEAD_DIM)
    grads = grad_group.reshape(length, heads_item, HEAD_DIM)
    grad_keys = jnp.zeros((length, heads_item, HEAD_DIM), jnp.float32)
    grad_values = jnp.zeros((length, heads_item, HEAD_DIM), jnp.float32)
    query_parts = []
    for start in range(0, length, block):
        q_rows = queries[start : start + block]
        g_rows = grads[start : start + block]
        scores = masked_scores(q_rows, keys, start, length_s, scale)
        probs = jnp.exp(scores - lse[:, start : start + block])
        grad_values = grad_values + jnp.einsum(
            "hqk,qhd->khd", probs.astype(jnp.bfloat16), g_rows, preferred_element_type=jnp.float32
        )
        grad_probs = jnp.einsum("qhd,khd->hqk", g_rows, values, preferred_element_type=jnp.float32)
        delta = jnp.sum(probs * grad_probs, axis=-1, keepdims=True)
        grad_scores = (probs * (grad_probs - delta)).astype(jnp.bfloat16)
        part = (
            jnp.einsum("hqk,khd->qhd", grad_scores, keys, preferred_element_type=jnp.float32)
            * scale
        )
        query_parts.append(part.reshape(block, width))
        grad_keys = (
            grad_keys
            + jnp.einsum("hqk,qhd->khd", grad_scores, q_rows, preferred_element_type=jnp.float32)
            * scale
        )
    return (
        jnp.concatenate(query_parts, axis=0),
        grad_keys.reshape(length, width),
        grad_values.reshape(length, width),
    )


def to_groups(matrix):
    length, width = matrix.shape
    return matrix.reshape(length, width // 128, 128).transpose(1, 0, 2)


def from_groups(stacked):
    count, length, width = stacked.shape
    return stacked.transpose(1, 0, 2).reshape(length, count * width)


def one_sequence(params, tokens_seq, grad_seq, length_s, weight_s):
    (
        w_qkv,
        w_out,
        w_up,
        w_down,
        bias_q,
        bias_v,
        bias_out,
        bias_up,
        bias_down,
        gain_one,
        shift_one,
        gain_two,
        shift_two,
    ) = params
    width = w_out.shape[0]
    length = tokens_seq.shape[0]
    g_one = gain_one.astype(jnp.float32)
    g_two = gain_two.astype(jnp.float32)
    inputs = tokens_seq.astype(jnp.float32)
    norm_one, rstd_one = norm_rows(inputs)
    a_one = (norm_one * g_one + shift_one.astype(jnp.float32)).astype(jnp.bfloat16)
    qkv = jnp.dot(a_one, w_qkv, preferred_element_type=jnp.float32)
    query = (qkv[:, :width] + bias_q.astype(jnp.float32)).astype(jnp.bfloat16)
    key_all = qkv[:, width : 2 * width].astype(jnp.bfloat16)
    value = (qkv[:, 2 * width :] + bias_v.astype(jnp.float32)).astype(jnp.bfloat16)
    q_groups, k_groups, v_groups = (to_groups(query), to_groups(key_all), to_groups(value))
    attended, lse = lax.map(
        lambda item: group_forward(item[0], item[1], item[2], length_s),
        (q_groups, k_groups, v_groups),
    )
    attended = from_groups(attended).astype(jnp.bfloat16)
    x_two = (
        inputs
        + jnp.dot(attended, w_out, preferred_element_type=jnp.float32)
        + bias_out.astype(jnp.float32)
    )
    norm_two, rstd_two = norm_rows(x_two)
    a_two = (norm_two * g_two + shift_two.astype(jnp.float32)).astype(jnp.bfloat16)
    hidden_pre = jnp.dot(a_two, w_up, preferred_element_type=jnp.float32) + bias_up.astype(
        jnp.float32
    )
    hidden = gelu_value(hidden_pre).astype(jnp.bfloat16)
    result = (
        x_two
        + jnp.dot(hidden, w_down, preferred_element_type=jnp.float32)
        + bias_down.astype(jnp.float32)
    )
    valid = (jnp.arange(length) < length_s).astype(jnp.float32)
    cotangent = grad_seq.astype(jnp.float32) * (weight_s * valid)[:, None]
    g_branch = cotangent.astype(jnp.bfloat16)
    grad_w_down = left_dot(hidden, g_branch)
    grad_bias_down = jnp.sum(g_branch.astype(jnp.float32), axis=0)
    grad_hidden = right_dot(g_branch, w_down)
    g_pre = (grad_hidden * gelu_slope(hidden_pre)).astype(jnp.bfloat16)
    grad_w_up = left_dot(a_two, g_pre)
    grad_bias_up = jnp.sum(g_pre.astype(jnp.float32), axis=0)
    grad_a_two = right_dot(g_pre, w_up)
    grad_gain_two = jnp.sum(grad_a_two * norm_two, axis=0)
    grad_shift_two = jnp.sum(grad_a_two, axis=0)
    grad_x_two = cotangent + norm_back(grad_a_two * g_two, norm_two, rstd_two)
    g_att = grad_x_two.astype(jnp.bfloat16)
    grad_w_out = left_dot(attended, g_att)
    grad_bias_out = jnp.sum(g_att.astype(jnp.float32), axis=0)
    g_attended = right_dot(g_att, w_out).astype(jnp.bfloat16)
    grad_q, grad_k, grad_v = lax.map(
        lambda item: group_backward(item[0], item[1], item[2], item[3], item[4], length_s),
        (q_groups, k_groups, v_groups, lse, to_groups(g_attended)),
    )
    grad_q = from_groups(grad_q).astype(jnp.bfloat16)
    grad_k = from_groups(grad_k).astype(jnp.bfloat16)
    grad_v = from_groups(grad_v).astype(jnp.bfloat16)
    grad_bias_q = jnp.sum(grad_q.astype(jnp.float32), axis=0)
    grad_bias_v = jnp.sum(grad_v.astype(jnp.float32), axis=0)
    grad_qkv_rows = jnp.concatenate([grad_q, grad_k, grad_v], axis=1)
    grad_w_qkv = left_dot(a_one, grad_qkv_rows)
    grad_a_one = right_dot(grad_qkv_rows, w_qkv)
    grad_gain_one = jnp.sum(grad_a_one * norm_one, axis=0)
    grad_shift_one = jnp.sum(grad_a_one, axis=0)
    grad_inputs = grad_x_two + norm_back(grad_a_one * g_one, norm_one, rstd_one)
    grads = (
        grad_w_qkv,
        grad_w_out,
        grad_w_up,
        grad_w_down,
        grad_bias_q,
        grad_bias_v,
        grad_bias_out,
        grad_bias_up,
        grad_bias_down,
        grad_gain_one,
        grad_shift_one,
        grad_gain_two,
        grad_shift_two,
    )
    return (result.astype(jnp.bfloat16), grad_inputs.astype(jnp.bfloat16), grads)


def body(
    tokens,
    grad_out,
    lengths,
    task_of,
    task_tokens,
    w_qkv,
    w_out,
    w_up,
    w_down,
    bias_q,
    bias_v,
    bias_out,
    bias_up,
    bias_down,
    gain_one,
    shift_one,
    gain_two,
    shift_two,
):
    params = (
        lax.all_gather(w_qkv, "dp", axis=0, tiled=True),
        lax.all_gather(w_out, "dp", axis=0, tiled=True),
        lax.all_gather(w_up, "dp", axis=0, tiled=True),
        lax.all_gather(w_down, "dp", axis=0, tiled=True),
        lax.all_gather(bias_q, "dp", axis=0, tiled=True),
        lax.all_gather(bias_v, "dp", axis=0, tiled=True),
        lax.all_gather(bias_out, "dp", axis=0, tiled=True),
        lax.all_gather(bias_up, "dp", axis=0, tiled=True),
        lax.all_gather(bias_down, "dp", axis=0, tiled=True),
        lax.all_gather(gain_one, "dp", axis=0, tiled=True),
        lax.all_gather(shift_one, "dp", axis=0, tiled=True),
        lax.all_gather(gain_two, "dp", axis=0, tiled=True),
        lax.all_gather(shift_two, "dp", axis=0, tiled=True),
    )
    matches = task_of[:, None] == jnp.arange(task_tokens.shape[0])[None, :]
    counted = jnp.sum(jnp.where(matches, task_tokens[None, :], 0), axis=1).astype(jnp.float32)
    weights = UNIT / counted
    start_sums = tuple((jnp.zeros(p.shape, jnp.float32) for p in params))

    def step(carry, item):
        tokens_seq, grad_seq, length_s, weight_s = item
        result, grad_inputs, grads = one_sequence(params, tokens_seq, grad_seq, length_s, weight_s)
        return (tuple((c + g for c, g in zip(carry, grads))), (result, grad_inputs))

    totals, (outputs, grads_in) = lax.scan(step, start_sums, (tokens, grad_out, lengths, weights))
    shares = jax.tree.map(
        lambda part: part.astype(jnp.float32),
        lax.psum_scatter(shortened(totals), "dp", scatter_dimension=0, tiled=True),
    )
    summed = jax.tree.map(lambda part: part.astype(jnp.float32), lax.psum(shortened(shares), "grp"))
    return (
        outputs,
        grads_in,
        summed[0],
        summed[1],
        summed[2],
        summed[3],
        summed[4],
        summed[5],
        summed[6],
        summed[7],
        summed[8],
        summed[9],
        summed[10],
        summed[11],
        summed[12],
    )


def solution(mesh):
    in_specs = (
        P(("grp", "dp"), None, None),
        P(("grp", "dp"), None, None),
        P(("grp", "dp")),
        P(("grp", "dp")),
        P(),
        P("dp", None),
        P("dp", None),
        P("dp", None),
        P("dp", None),
        P("dp"),
        P("dp"),
        P("dp"),
        P("dp"),
        P("dp"),
        P("dp"),
        P("dp"),
        P("dp"),
        P("dp"),
    )
    out_specs = (
        P(("grp", "dp"), None, None),
        P(("grp", "dp"), None, None),
        P("dp", None),
        P("dp", None),
        P("dp", None),
        P("dp", None),
        P("dp"),
        P("dp"),
        P("dp"),
        P("dp"),
        P("dp"),
        P("dp"),
        P("dp"),
        P("dp"),
        P("dp"),
    )
    return jax.shard_map(body, mesh=mesh, in_specs=in_specs, out_specs=out_specs, check_vma=False)
```

profile of v0, /device:TPU:0, one launch (start us, length us, event | category | flops | bytes accessed | tf_op | source)
XLA Modules:
  0.0 589.8 jit_solution(6816034550922484683)
XLA Ops:
  21.8 25.9 %all-reduce.18 = (bf16[768]{0:T(1024)(128)(2,1)S(1)}, bf16[768]{0:T(1024)(128)(2,1)S(1)}, bf16[768]{0:T(1024)(128)(2,1)S(1)}, bf16[768]{0:T(1024)(128)(2,1)S(1)}...) all-reduce(bf16[768]{0:T(1024)(128)(2,1)S(1)} %dynamic-update-slice, ...), channel_id=1, replica_groups=mesh['grp'=4,'dp'=8] {'dp'}, use_global_device_ids=true, to_apply=%add.1 | all-reduce | flops 5376 | bytes 21504
  47.8 8.0 %all-gather = bf16[8,1,384]{2,1,0:T(2,128)(2,1)S(1)} all-gather(bf16[1,1,384]{2,1,0:T(2,128)(2,1)S(1)} %reshape.381), channel_id=1, replica_groups=mesh['grp'=4,'dp'=8] {'dp'}, dimensions={0}, use_global_device_ids=true | all-gather | bytes 6912 | tf_op jit(solution)/shard_map/all_gather | solution.py:261
  60.1 6.3 %fusion.74 = f32[1024,2304]{1,0:T(8,128)S(1)} fusion(bf16[768,2304]{1,0:T(8,128)(2,1)} %all-gather.6.cloned.1.call-done, bf16[1,1024,768]{1,2,0:T(8,128)(2,1)S(1)} %copy.57, f32[768]{0:T(1024)S(1)} %convert_element_type.271, f32[768]{0:T(1024)S(1)} %convert_element_type.270, f32[1024]{0:T(1024)S(1)} %add_rsqrt_fusion.1, f32[1024]{0:T(1024)S(1)} %broadcast_multiply_fusion.5), kind=kOutput, calls=%fused_computation.144 | convolution fusion | flops 3628597248 | bytes 14563328 | tf_op jit(solution)/shard_map/while/body/eval_jaxpr/dot_general | solution.py:157
  67.7 2.3 fusion.58
  71.8 2.6 copy.60
  74.4 2.6 copy.59
  78.3 66.7 %while.35 = (s32[]{:T(128)}, bf16[6,1024,128]{1,2,0:T(8,128)(2,1)}, f32[6,2,1024,1]{2,1,3,0:T(2,128)S(1)}, bf16[6,1024,128]{1,2,0:T(8,128)(2,1)S(1)}, s32[]{:T(1...) while((s32[]{:T(128)}, bf16[6,1024,128]{1,2,0:T(8,128)(2,1)}, ...), condition=%wide.region_7.8_spmd, body=%wide.region_2.7_spmd.sunk | while | flops 562562560 | bytes 33110160 | solution.py:162
  145.0 4.0 fusion.79
  151.1 14.0 %multiply_convert_fusion.2 = (bf16[1024,3072]{1,0:T(8,128)(2,1)}, f32[1024,3072]{1,0:T(8,128)}) fusion(f32[3072]{0:T(1024)S(1)} %bitcast.310, bf16[768,3072]{1,0:T(8,128)(2,1)} %all-gather.10.cloned.1.call-done, f32[1024,768]{0,1:T(8,128)} %copy-done.2, f32[768]{0:T(1024)S(1)} %convert_element_type.282, f32[768]{0:T(1024)S(1)} %convert_element_type.281, ...), kind=kOutput, calls=%fused_computation.79 | convolution fusion | flops 4854644736 | bytes 26765312 | tf_op jit(solution)/shard_map/while/body/eval_jaxpr/dot_general | solution.py:174
  165.1 12.8 %fusion.80 = (bf16[3072]{0:T(1024)(128)(2,1)}, bf16[1024,3072]{1,0:T(8,128)(2,1)S(1)}) fusion(f32[1024,3072]{1,0:T(8,128)} %get-tuple-element.366, f32[3072]{0:T(1024)S(1)} %bitcast.311, bf16[3072,768]{1,0:T(8,128)(2,1)} %all-gather.12.cloned.1.call-done, bf16[1,1024,768]{1,2,0:T(8,128)(2,1)S(1)} %copy-done.7, f32[1024]{0:T(1024)S(1)} %fusion.67), kind=kOutput, calls=%fused_computation.148 | convolution fusion | flops 4871943168 | bytes 25188352 | tf_op jit(solution)/shard_map/while/body/eval_jaxpr/dot_general | solution.py:49
  177.9 7.3 %fusion.82 = (bf16[768]{0:T(1024)(128)(2,1)}, f32[1024,768]{1,0:T(8,128)}) fusion(bf16[1024,3072]{1,0:T(8,128)(2,1)S(1)} %get-tuple-element.360, bf16[768,3072]{1,0:T(8,128)(2,1)S(1)} %copy-done.27), kind=kOutput, calls=%fused_computation.150 | convolution fusion | flops 4832623616 | bytes 14157312 | tf_op jit(solution)/shard_map/while/body/eval_jaxpr/dot_general | solution.py:49
  185.2 3.9 copy.63
  189.2 3.6 multiply_reduce_fusion.2
  192.8 2.3 convert_reduce_fusion.1
  196.8 2.4 convolution_convert_fusion.4
  199.4 4.4 convolution_convert_fusion.3
  206.7 117.5 %while.36 = (s32[]{:T(128)}, bf16[6,1024,128]{1,2,0:T(8,128)(2,1)}, bf16[6,1024,128]{1,2,0:T(8,128)(2,1)}, bf16[6,1024,128]{1,2,0:T(8,128)(2,1)S(1)}, bf16[6,102...) while((s32[]{:T(128)}, bf16[6,1024,128]{1,2,0:T(8,128)(2,1)}, ...), condition=%wide.region_16.17_spmd, body=%wide.region_13.16_spmd.sunk | while | flops 1377172992 | bytes 76363952 | solution.py:200
  324.3 7.8 %convolution_convert_fusion.2 = bf16[768,2304]{1,0:T(8,128)(2,1)} fusion(bf16[1024,768]{0,1:T(8,128)(2,1)S(1)} %bitcast.295, bf16[1024,768]{0,1:T(8,128)(2,1)} %bitcast.303, bf16[1024,768]{0,1:T(8,128)(2,1)} %bitcast.297, bf16[1,1024,768]{1,2,0:T(8,128)(2,1)S(1)} %copy-done.1, f32[768]{0:T(1024)S(1)} %copy-done.25, f32[768]{0:T(1024)S(1)} %copy-done.15, ...), kind=kOutput, calls=%fused_computation.83 | convolution fusion | flops 3644522496 | bytes 9844736 | tf_op jit(solution)/shard_map/while/body/eval_jaxpr/dot_general | solution.py:43
  332.7 9.9 %convolution_convert_fusion.1 = bf16[768,3072]{1,0:T(8,128)(2,1)} fusion(bf16[1024,3072]{1,0:T(8,128)(2,1)} %copy-done.30, f32[1024,768]{0,1:T(8,128)} %copy-done.2, f32[768]{0:T(1024)S(1)} %copy-done.23, f32[768]{0:T(1024)S(1)} %convert_element_type.281, f32[1024]{0:T(1024)S(1)} %add_rsqrt_fusion, f32[1024]{0:T(1024)S(1)} %broadcast_multiply_fusion.4), kind=kOutput, calls=%fused_computation.82 | convolution fusion | flops 4838129664 | bytes 14170112 | tf_op jit(solution)/shard_map/while/body/eval_jaxpr/dot_general | solution.py:43
  342.7 9.5 %convolution_convert_fusion = bf16[3072,768]{1,0:T(8,128)(2,1)} fusion(bf16[1024,3072]{1,0:T(8,128)(2,1)} %get-tuple-element.365, bf16[1,1024,768]{1,2,0:T(8,128)(2,1)} %copy.62, f32[1024]{0:T(1024)S(1)} %fusion.67), kind=kOutput, calls=%fused_computation.81 | convolution fusion | flops 4836556800 | bytes 12587008 | tf_op jit(solution)/shard_map/while/body/eval_jaxpr/dot_general | solution.py:43
  356.1 8.4 %fusion.81 = (bf16[768]{0:T(1024)(128)(2,1)S(1)}, f32[1024,768]{1,0:T(8,128)}) fusion(bf16[768,2304]{1,0:T(8,128)(2,1)} %all-gather.6.cloned.1.call-done, bf16[1024,768]{0,1:T(8,128)(2,1)S(1)} %bitcast.296, bf16[1024,768]{0,1:T(8,128)(2,1)} %bitcast.304, bf16[1024,768]{0,1:T(8,128)(2,1)} %bitcast.298), kind=kOutput, calls=%fused_computation.149 | convolution fusion | flops 3638820096 | bytes 11404800 | tf_op jit(solution)/shard_map/while/body/eval_jaxpr/dot_general | solution.py:49
  364.5 3.7 copy.64
  368.3 2.9 fusion.54
  371.2 23.9 %all-reduce.17 = (bf16[768]{0:T(1024)(128)(2,1)S(1)}, bf16[768]{0:T(1024)(128)(2,1)S(1)}, bf16[768]{0:T(1024)(128)(2,1)S(1)}, bf16[768]{0:T(1024)(128)(2,1)S(1)}...) all-reduce(bf16[768]{0:T(1024)(128)(2,1)S(1)} %dynamic-update-slice, ...), channel_id=1, replica_groups=mesh['grp'=4,'dp'=8] {'dp'}, use_global_device_ids=true, to_apply=%add.7 | all-reduce | flops 9984 | bytes 39936
  395.2 43.3 %reduce-scatter.9.cloned.1.call-done = bf16[96,3072]{1,0:T(8,128)(2,1)} async-done(((bf16[768,3072]{1,0:T(8,128)(2,1)}), bf16[96,3072]{1,0:T(8,128)(2,1)}) %reduce-scatter.9.cloned.1.call-update) | async-done | bytes 589840 | tf_op jit(solution)/shard_map/reduce_scatter | solution.py:281
  438.5 57.4 %reduce-scatter.11.cloned.1.call-done = bf16[384,768]{1,0:T(8,128)(2,1)} async-done(((bf16[3072,768]{1,0:T(8,128)(2,1)}), bf16[384,768]{1,0:T(8,128)(2,1)}) %reduce-scatter.11.cloned.1.call-update) | async-done | bytes 589840 | tf_op jit(solution)/shard_map/reduce_scatter | solution.py:281
  495.9 9.1 %fusion.63 = bf16[1,1024,768]{1,2,0:T(8,128)(2,1)S(1)} fusion(f32[768]{0:T(1024)S(1)} %convert_element_type.286, f32[1024,768]{0,1:T(8,128)} %copy-done.2, bf16[1024,3072]{1,0:T(8,128)(2,1)} %get-tuple-element.365, bf16[3072,768]{1,0:T(8,128)(2,1)} %all-gather.12.cloned.1.call-done), kind=kOutput, calls=%fused_computation.125 | convolution fusion | flops 4834197504 | bytes 15731712 | tf_op jit(solution)/shard_map/while/body/eval_jaxpr/dot_general | solution.py:180
  505.7 12.4 %all-reduce.19 = (bf16[96]{0:T(256)(128)(2,1)S(1)}, bf16[96]{0:T(256)(128)(2,1)S(1)}, bf16[96]{0:T(256)(128)(2,1)S(1)}, bf16[384]{0:T(512)(128)(2,1)S(1)}, bf16[...) all-reduce(bf16[96]{0:T(256)(128)(2,1)S(1)} %dynamic-slice.9, ...), channel_id=1, replica_groups=mesh['grp'=4,'dp'=8] {'grp'}, use_global_device_ids=true, to_apply=%region_29.30 | all-reduce | flops 1152 | bytes 4608 | tf_op jit(solution)/shard_map/psum | solution.py:283
  524.4 3.9 fusion.62
  529.9 46.0 %all-reduce.23.cloned.1.call-done = (bf16[96,2304]{1,0:T(8,128)(2,1)}, bf16[96,768]{1,0:T(8,128)(2,1)}, bf16[96,3072]{1,0:T(8,128)(2,1)}, bf16[384,768]{1,0:T(8,128)(2,1)}) async-done(((bf16[96,2304]{1,0:T(8,128)(2,1)}, bf16[96,768]{1,0:T(8,128)(2,1)}, bf16[96,3072]{1,0:T(8,128)(2,1)}, bf16[384,768]{1,0:T(8,128)(2,1)}), (bf16[96,2304]{1,0:T(8,128)(2,1)}, bf16[96,768]{1,0:T(8,128)(2,1)}, ...) | async-done | bytes 1769488 | tf_op jit(solution)/shard_map/psum | solution.py:283
  577.6 2.0 convert_element_type.306
  579.6 2.2 convert_element_type.310
  (386 shorter events, 224.9 us)
Async XLA Ops:
  7.2 52.9 %all-gather.6.cloned.1.call-start = ((), (), s32[]{:S(2)}) async-start(), calls=%async_computation.4 | async-start | bytes 3981312 | tf_op jit(solution)/shard_map/all_gather | solution.py:254
  7.9 137.1 %all-gather.8.cloned.1.call-start = ((), (), s32[]{:S(2)}) async-start(), calls=%async_computation.5 | async-start | bytes 1327104 | tf_op jit(solution)/shard_map/all_gather | solution.py:255
  8.7 142.4 %all-gather.10.cloned.1.call-start = ((), (), s32[]{:S(2)}) async-start(), calls=%async_computation.6 | async-start | bytes 5308416 | tf_op jit(solution)/shard_map/all_gather | solution.py:256
  9.4 155.7 %all-gather.12.cloned.1.call-start = ((), (), s32[]{:S(2)}) async-start(), calls=%async_computation.7 | async-start | bytes 5308416 | tf_op jit(solution)/shard_map/all_gather | solution.py:257
  10.0 385.2 %reduce-scatter.7.cloned.1.call-start = ((), (), s32[]{:S(2)}) async-start(), calls=%async_computation.9 | async-start | bytes 1327104 | tf_op jit(solution)/shard_map/reduce_scatter | solution.py:281
  47.7 12.4 %copy-start.24 = (f32[768]{0:T(1024)}, f32[768]{0:T(1024)S(1)}, u32[]{:S(2)}) copy-start(f32[768]{0:T(1024)S(1)} %convert_element_type.271) | copy-start | bytes 9220
  47.7 12.4 %copy-start.14 = (f32[768]{0:T(1024)}, f32[768]{0:T(1024)S(1)}, u32[]{:S(2)}) copy-start(f32[768]{0:T(1024)S(1)} %convert_element_type.270) | copy-start | bytes 9220
  47.7 103.3 %copy-start.22 = (f32[768]{0:T(1024)}, f32[768]{0:T(1024)S(1)}, u32[]{:S(2)}) copy-start(f32[768]{0:T(1024)S(1)} %convert_element_type.282) | copy-start | bytes 9220
  57.6 87.4 %copy-start = (bf16[1,1024,768]{1,2,0:T(8,128)(2,1)}, bf16[1,1024,768]{1,2,0:T(8,128)(2,1)S(1)}, u32[]{:S(2)}) copy-start(bf16[1,1024,768]{1,2,0:T(8,128)(2,1)S(1)} %copy.57) | copy-start | bytes 4718596
  57.9 8.5 %copy-start.12 = (f32[1024]{0:T(1024)}, f32[1024]{0:T(1024)S(1)}, u32[]{:S(2)}) copy-start(f32[1024]{0:T(1024)S(1)} %broadcast_multiply_fusion.5) | copy-start | bytes 12292
  58.4 8.0 %copy-start.16 = (f32[1024]{0:T(1024)}, f32[1024]{0:T(1024)S(1)}, u32[]{:S(2)}) copy-start(f32[1024]{0:T(1024)S(1)} %add_rsqrt_fusion.1) | copy-start | bytes 12292
  145.0 4.0 copy-start.6
  151.1 14.0 %copy-start.7 = (bf16[1,1024,768]{1,2,0:T(8,128)(2,1)S(1)}, bf16[1,1024,768]{1,2,0:T(8,128)(2,1)}, u32[]{:S(2)}) copy-start(bf16[1,1024,768]{1,2,0:T(8,128)(2,1)} %copy.62) | copy-start | bytes 4718596
  165.1 12.8 %copy-start.27 = (bf16[768,3072]{1,0:T(8,128)(2,1)S(1)}, bf16[768,3072]{1,0:T(8,128)(2,1)}, u32[]{:S(2)}) copy-start(bf16[768,3072]{1,0:T(8,128)(2,1)} %all-gather.10.cloned.1.call-done) | copy-start | bytes 14155780
  177.9 7.4 %copy-start.30 = (bf16[1024,3072]{1,0:T(8,128)(2,1)}, bf16[1024,3072]{1,0:T(8,128)(2,1)S(1)}, u32[]{:S(2)}) copy-start(bf16[1024,3072]{1,0:T(8,128)(2,1)S(1)} %get-tuple-element.360) | copy-start | bytes 18874372
  185.2 3.9 copy-start.3
  189.1 3.6 copy-start.4
  189.2 3.6 copy-start.8
  192.8 4.0 copy-start.10
  199.3 195.9 %reduce-scatter.5.cloned.1.call-start = ((), (), s32[]{:S(2)}) async-start(), calls=%async_computation.8 | async-start | bytes 3981312 | tf_op jit(solution)/shard_map/reduce_scatter | solution.py:281
  206.7 117.6 %copy-start.1 = (bf16[1,1024,768]{1,2,0:T(8,128)(2,1)S(1)}, bf16[1,1024,768]{1,2,0:T(8,128)(2,1)}, u32[]{:S(2)}) copy-start(bf16[1,1024,768]{1,2,0:T(8,128)(2,1)} %copy-done) | copy-start | bytes 4718596
  206.7 117.6 %copy-start.13 = (f32[1024]{0:T(1024)S(1)}, f32[1024]{0:T(1024)}, u32[]{:S(2)}) copy-start(f32[1024]{0:T(1024)} %copy-done.12) | copy-start | bytes 12292
  206.7 117.6 %copy-start.15 = (f32[768]{0:T(1024)S(1)}, f32[768]{0:T(1024)}, u32[]{:S(2)}) copy-start(f32[768]{0:T(1024)} %copy-done.14) | copy-start | bytes 9220
  206.7 117.6 %copy-start.17 = (f32[1024]{0:T(1024)S(1)}, f32[1024]{0:T(1024)}, u32[]{:S(2)}) copy-start(f32[1024]{0:T(1024)} %copy-done.16) | copy-start | bytes 12292
  206.7 117.6 %copy-start.25 = (f32[768]{0:T(1024)S(1)}, f32[768]{0:T(1024)}, u32[]{:S(2)}) copy-start(f32[768]{0:T(1024)} %copy-done.24) | copy-start | bytes 9220
  332.1 106.4 %reduce-scatter.9.cloned.1.call-start = ((), (), s32[]{:S(2)}) async-start(), calls=%async_computation.10 | async-start | bytes 5308416 | tf_op jit(solution)/shard_map/reduce_scatter | solution.py:281
  342.6 153.3 %reduce-scatter.11.cloned.1.call-start = ((), (), s32[]{:S(2)}) async-start(), calls=%async_computation.11 | async-start | bytes 5308416 | tf_op jit(solution)/shard_map/reduce_scatter | solution.py:281
  352.2 223.7 %all-reduce.23.cloned.1.call-start = ((), (), s32[]{:S(2)}) async-start(), calls=%async_computation.12 | async-start | bytes 3538944 | tf_op jit(solution)/shard_map/psum | solution.py:283
  368.2 3.0 copy-start.20
  368.2 3.0 copy-start.21
  368.2 3.0 copy-start.26
  575.9 5.9 copy-start.11
  (8 other events, 16.5 us)
Sparse Core Ops, SparseCore 0:
  9.9 36.8 all-gather.5
  48.7 24.0 all-gather.7
  74.6 38.9 all-gather.9
  115.4 38.8 all-gather.11
  199.4 37.0 reduce-scatter.6
  332.2 48.4 reduce-scatter.4
  384.6 53.8 reduce-scatter.8
  441.9 53.8 reduce-scatter.10
  498.7 77.1 all-reduce.22
where the time goes:
time: 599 us; the launch traced here: 590 us
  matrix products  185 us (31%)
  waiting for transfers between devices  149 us (25%)
  other arithmetic  84.5 us (14%)
  local copies, waits for them, and re-layouts  79.9 us (13%)
  blocking collectives  70.2 us (12%)
  between operations  18.8 us (3%)
    reduce_scatter x4, waiting for transfers between devices, body(): lax.psum_scatter(shortened(totals), 'dp', scatter_dimension=0, tiled=True)  101 us
    unnamed x2, blocking collectives  49.8 us
    psum x1, waiting for transfers between devices, body(): lax.psum(shortened(shares), 'grp')  46 us
    dot_general x4, matrix products, right_dot(): lax.dot_general(left, right, (((1,), (1,)), ((), ())), preferred_element_...  33 us
    dot_general x4, matrix products, left_dot(): lax.dot_general(left, right, (((0,), (0,)), ((), ())), preferred_element_...  29.6 us
    dot_general x24, matrix products, masked_scores(): jnp.einsum('qhd,khd->hqk', q_rows, keys, preferred_element_type=jnp.float32)  22 us
    dot_general x12, matrix products, group_backward(): jnp.einsum('qhd,khd->hqk', g_rows, values, preferred_element_type=jnp.flo...  21.2 us
    unnamed x93, local copies, waits for them, and re-layouts  19.7 us
  transfers between devices with their start and end apart: 9, of which 3 were waited for; matrix products, arithmetic and copies ran while one was open for 52% of the time, Pallas kernels for 0%

commit v1 on v0

v1 whole, which is shorter than its diff:
```python
import functools
import math

import jax
import jax.numpy as jnp
from jax import lax
from jax.experimental import pallas as pl
from jax.experimental.pallas import tpu as pltpu
from jax.sharding import PartitionSpec as P

F32 = jnp.float32
BF16 = jnp.bfloat16
EPS = 1e-05
UNIT = 1024.0
HEAD = 64
BLOCK = 256
TILE = 512
BQ, BV, BO, BD, G1, S1, G2, S2, UP = range(9)
VEC_ROWS = 16


def dot(left, right, left_dim, right_dim):
    return lax.dot_general(
        left, right, (((left_dim,), (right_dim,)), ((), ())), preferred_element_type=F32
    )


def nn(left, right):
    return dot(left, right, 1, 0)


def nt(left, right):
    return dot(left, right, 1, 1)


def tn(left, right):
    return dot(left, right, 0, 0)


def norm_rows(values):
    mean = jnp.mean(values, axis=-1, keepdims=True)
    centered = values - mean
    rstd = lax.rsqrt(jnp.mean(centered * centered, axis=-1, keepdims=True) + EPS)
    return centered * rstd, rstd


def norm_back(grad_norm, normed, rstd):
    mean_one = jnp.mean(grad_norm, axis=-1, keepdims=True)
    mean_two = jnp.mean(grad_norm * normed, axis=-1, keepdims=True)
    return rstd * (grad_norm - mean_one - normed * mean_two)


def column_sum(values):
    return jnp.sum(values, axis=0, keepdims=True)


def rows_at(index, size=BLOCK):
    return pl.ds(pl.multiple_of(index * size, size), size)


def norm_one_phase(x, vecs, a1):
    gain, shift = vecs[G1 : G1 + 1, :], vecs[S1 : S1 + 1, :]

    def step(i, _):
        at = rows_at(i)
        normed, _ = norm_rows(x[at, :].astype(F32))
        a1[at, :] = (normed * gain + shift).astype(BF16)
        return 0

    lax.fori_loop(0, x.shape[0] // BLOCK, step, 0)


def qkv_phase(j, a1, wqkv, vecs, k, v, q_t, k_t, v_t):
    at = rows_at(j)
    values = nn(a1[...], wqkv[j])
    bias_q, bias_v = vecs[BQ : BQ + 1, at], vecs[BV : BV + 1, at]
    query = (values[:, :BLOCK] + bias_q).astype(BF16) * (HEAD**-0.5)
    key_all = values[:, BLOCK : 2 * BLOCK].astype(BF16)
    value = (values[:, 2 * BLOCK :] + bias_v).astype(BF16)
    k[:, at] = key_all
    v[:, at] = value
    q_t[at, :] = query.T
    k_t[at, :] = key_all.T
    v_t[at, :] = value.T


def padded(rows, side):
    zeros = jnp.zeros_like(rows)
    return jnp.concatenate([rows, zeros] if side == 0 else [zeros, rows], axis=0)


def attend_pair(p, length_s, k, q_t, v_t, o_t, o, lse):
    length = k.shape[0]
    lanes = rows_at(p, 2 * HEAD)
    for i in range(length // BLOCK):
        cols = slice(i * BLOCK, (i + 1) * BLOCK)
        seen = (i + 1) * BLOCK
        queries = i * BLOCK + lax.broadcasted_iota(jnp.int32, (1, BLOCK), 1)
        limit = jnp.minimum(queries + 1, length_s)
        key_index = lax.broadcasted_iota(jnp.int32, (seen, BLOCK), 0)
        allowed = key_index < limit
        halves = []
        for side in range(2):
            head = 2 * p + side
            at = rows_at(head, HEAD)
            scores = nn(k[:seen, lanes], padded(q_t[at, cols], side))
            scores = jnp.where(allowed, scores, -1e30)
            top = jnp.max(scores, axis=0, keepdims=True)
            weights = jnp.exp(scores - top)
            total = jnp.sum(weights, axis=0, keepdims=True)
            lse[head, :, cols] = jnp.where(queries < length_s, top + jnp.log(total), 1e30)
            result = nn(v_t[at, :seen], weights.astype(BF16)) * (1.0 / total)
            halves.append(result.astype(BF16))
        both = jnp.concatenate(halves, axis=0)
        o_t[lanes, cols] = both
        o[cols, lanes] = both.T


def attend_back_pair(p, k, v, q_t, k_t, g_o_t, lse, delta, dk_t, dv_t, dqkv, gvec):
    length = k.shape[0]
    count = length // BLOCK
    lanes = rows_at(p, 2 * HEAD)
    dq_sides = []
    for side in range(2):
        head = 2 * p + side
        at = rows_at(head, HEAD)
        here = slice(side * HEAD, (side + 1) * HEAD)
        dq_parts = []
        for i in reversed(range(count)):
            cols = slice(i * BLOCK, (i + 1) * BLOCK)
            seen = (i + 1) * BLOCK
            q_cols, g_cols = q_t[at, cols], g_o_t[at, cols]
            scores = nn(k[:seen, lanes], padded(q_cols, side))
            key_index = lax.broadcasted_iota(jnp.int32, (BLOCK, BLOCK), 0)
            query_index = lax.broadcasted_iota(jnp.int32, (BLOCK, BLOCK), 1)
            diagonal = jnp.where(key_index <= query_index, scores[seen - BLOCK :], -1e30)
            if i > 0:
                scores = jnp.concatenate([scores[: seen - BLOCK], diagonal], axis=0)
            else:
                scores = diagonal
            probs = jnp.exp(scores - lse[head, :, cols])
            grad_probs = nn(v[:seen, lanes], padded(g_cols, side))
            grad_scores = (probs * (grad_probs - delta[head, :, cols])).astype(BF16)
            part_v = nt(g_cols, probs.astype(BF16))
            part_k = nt(q_cols, grad_scores)
            if i == count - 1:
                dv_t[here, :] = part_v
                dk_t[here, :] = part_k
            else:
                dv_t[here, :seen] += part_v
                dk_t[here, :seen] += part_k
            dq_parts.append(nn(k_t[at, :seen], grad_scores) * (HEAD**-0.5))
        dq_sides.append(jnp.concatenate(dq_parts[::-1], axis=1).astype(BF16))
    dq = jnp.concatenate(dq_sides, axis=0).T
    dk = dk_t[...].astype(BF16).T
    dv = dv_t[...].astype(BF16).T
    base = lax.rem(p, 2) * (2 * HEAD)
    for part, value in enumerate((dq, dk, dv)):
        place = pl.ds(pl.multiple_of(base + part * BLOCK, 2 * HEAD), 2 * HEAD)
        dqkv[:, place] = value
    gvec[BQ : BQ + 1, lanes] = column_sum(dq.astype(F32))
    gvec[BV : BV + 1, lanes] = column_sum(dv.astype(F32))


def norm_two_phase(x, o, wout, vecs, x2, a2, out_acc):
    bias, down = vecs[BO : BO + 1, :], vecs[BD : BD + 1, :]
    gain, shift = vecs[G2 : G2 + 1, :], vecs[S2 : S2 + 1, :]

    def step(i, _):
        at = rows_at(i)
        value = x[at, :].astype(F32) + nn(o[at, :], wout[...]) + bias
        x2[at, :] = value
        out_acc[at, :] = value + down
        normed, _ = norm_rows(value)
        a2[at, :] = (normed * gain + shift).astype(BF16)
        return 0

    lax.fori_loop(0, x.shape[0] // BLOCK, step, 0)


def cotangent_rows(i, grad_out, length_s, weight_s):
    at = rows_at(i)
    index = i * BLOCK + lax.broadcasted_iota(jnp.int32, (BLOCK, 1), 0)
    scale = jnp.where(index < length_s, weight_s, 0.0)
    return grad_out[at, :].astype(F32) * scale


def branch_phase(grad_out, length_s, weight_s, g_f, gvec):
    def step(i, total):
        rounded = cotangent_rows(i, grad_out, length_s, weight_s).astype(BF16)
        g_f[rows_at(i), :] = rounded
        return total + column_sum(rounded.astype(F32))

    width = grad_out.shape[1]
    total = lax.fori_loop(0, grad_out.shape[0] // BLOCK, step, jnp.zeros((1, width), F32))
    gvec[BD : BD + 1, :] = total


def hidden_tile(t, a2, g_f, wup, wdn, vecs, out_acc, da2, hr, gu, gvec):
    length = a2.shape[0]
    up, down = wup[t], wdn[t]
    bias = vecs[pl.ds(UP + t, 1), :TILE]
    total = jnp.zeros((1, TILE), F32)
    for m in range(length // BLOCK):
        at = slice(m * BLOCK, (m + 1) * BLOCK)
        u = nn(a2[at, :], up) + bias
        dh = nt(g_f[at, :], down)
        cdf = 0.5 + 0.5 * lax.erf(u * (1.0 / math.sqrt(2.0)))
        slope = cdf + u * (jnp.exp(-0.5 * u * u) * (1.0 / math.sqrt(2.0 * math.pi)))
        hidden = (u * cdf).astype(BF16)
        g_u = (dh * slope).astype(BF16)
        hr[at, :] = hidden
        gu[at, :] = g_u
        total = total + column_sum(g_u.astype(F32))
        out_acc[at, :] += nn(hidden, down)
        da2[at, :] += nt(g_u, up)
    gvec[pl.ds(UP + t, 1), :TILE] = total


def norm_two_back(grad_out, length_s, weight_s, x2, da2, vecs, g_a, gvec, out_acc, act):
    gain = vecs[G2 : G2 + 1, :]
    width = x2.shape[1]

    def step(i, carry):
        at = rows_at(i)
        act[at, :] = out_acc[at, :].astype(BF16)
        normed, rstd = norm_rows(x2[at, :])
        grad = da2[at, :]
        dx2 = cotangent_rows(i, grad_out, length_s, weight_s) + norm_back(grad * gain, normed, rstd)
        da2[at, :] = dx2
        rounded = dx2.astype(BF16)
        g_a[at, :] = rounded
        return (
            carry[0] + column_sum(grad * normed),
            carry[1] + column_sum(grad),
            carry[2] + column_sum(rounded.astype(F32)),
        )

    zero = jnp.zeros((1, width), F32)
    sums = lax.fori_loop(0, x2.shape[0] // BLOCK, step, (zero, zero, zero))
    gvec[G2 : G2 + 1, :], gvec[S2 : S2 + 1, :], gvec[BO : BO + 1, :] = sums


def attended_back(wout, g_a, o_t, g_o_t, delta):
    for i in range(g_a.shape[0] // BLOCK):
        cols = slice(i * BLOCK, (i + 1) * BLOCK)
        grad = nt(wout[...], g_a[cols, :]).astype(BF16)
        g_o_t[:, cols] = grad
        product = grad.astype(F32) * o_t[:, cols].astype(F32)
        for head in range(wout.shape[0] // HEAD):
            delta[head, :, cols] = column_sum(product[head * HEAD : (head + 1) * HEAD])


def norm_one_back(x, dx2, da1, vecs, gvec, input_grad):
    gain = vecs[G1 : G1 + 1, :]
    width = x.shape[1]

    def step(i, carry):
        at = rows_at(i)
        normed, rstd = norm_rows(x[at, :].astype(F32))
        grad = da1[at, :]
        result = dx2[at, :] + norm_back(grad * gain, normed, rstd)
        input_grad[at, :] = result.astype(BF16)
        return (carry[0] + column_sum(grad * normed), carry[1] + column_sum(grad))

    zero = jnp.zeros((1, width), F32)
    sums = lax.fori_loop(0, x.shape[0] // BLOCK, step, (zero, zero))
    gvec[G1 : G1 + 1, :], gvec[S1 : S1 + 1, :] = sums


def task_weight(task_of, task_tokens):
    return UNIT / task_tokens[task_of[0]].astype(F32)


def layer_body(comm, lengths, task_of, task_tokens, x, grad_out, act, input_grad, w, s):
    length_s = lengths[0]
    weight_s = task_weight(task_of, task_tokens)
    wqkv, wout, wup, wdn, vecs = w
    s.gvec[...] = jnp.zeros_like(s.gvec)
    s.da2[...] = jnp.zeros_like(s.da2)
    comm.begin()
    norm_one_phase(x, vecs, s.a1)
    branch_phase(grad_out, length_s, weight_s, s.g_f, s.gvec)

    def forward(j, _):
        comm.need_qkv(j)
        qkv_phase(j, s.a1, wqkv, vecs, s.k, s.v, s.q_t, s.k_t, s.v_t)

        def pair(p, _):
            attend_pair(2 * j + p, length_s, s.k, s.q_t, s.v_t, s.o_t, s.o, s.lse)
            return 0

        return lax.fori_loop(0, 2, pair, 0)

    lax.fori_loop(0, wqkv.shape[0], forward, 0)
    comm.need_out()
    norm_two_phase(x, s.o, wout, vecs, s.x2, s.a2, s.out_acc)

    def hidden(t, _):
        comm.need_hidden(t)
        hidden_tile(t, s.a2, s.g_f, wup, wdn, vecs, s.out_acc, s.da2, s.hr, s.gu, s.gvec)
        comm.give_up(t, lambda: tn(s.a2[...], s.gu[...]).astype(BF16))
        comm.give_down(t, lambda: tn(s.hr[...], s.g_f[...]).astype(BF16))
        return 0

    lax.fori_loop(0, wup.shape[0], hidden, 0)
    norm_two_back(
        grad_out, length_s, weight_s, s.x2, s.da2, vecs, s.a2, s.gvec, s.out_acc, s.g_f
    )
    act_copy = pltpu.make_async_copy(s.g_f, act, s.local.at[0])
    act_copy.start()
    comm.give_out(lambda: tn(s.o[...], s.a2[...]).astype(BF16))
    attended_back(wout, s.a2, s.o_t, s.g_o_t, s.delta)
    da1 = s.out_acc
    da1[...] = jnp.zeros_like(da1)

    def backward(j, _):
        def pair(p, _):
            attend_back_pair(
                2 * j + p, s.k, s.v, s.q_t, s.k_t, s.g_o_t, s.lse, s.delta,
                s.dk_t, s.dv_t, s.dqkv, s.gvec,
            )
            return 0

        lax.fori_loop(0, 2, pair, 0)
        comm.give_qkv(j, lambda: tn(s.a1[...], s.dqkv[...]).astype(BF16))
        for m in range(x.shape[0] // BLOCK):
            at = slice(m * BLOCK, (m + 1) * BLOCK)
            da1[at, :] += nt(s.dqkv[at, :], wqkv[j])
        return 0

    lax.fori_loop(0, wqkv.shape[0], backward, 0)
    norm_one_back(x, s.da2, da1, vecs, s.gvec, s.a1)
    grad_copy = pltpu.make_async_copy(s.a1, input_grad, s.local.at[1])
    grad_copy.start()
    comm.end()
    act_copy.wait()
    grad_copy.wait()


class Named:
    def __init__(self, names, refs):
        for name, ref in zip(names, refs):
            setattr(self, name, ref)


def layer_scratch(length, width):
    heads = width // HEAD
    wide, tall = (length, width), (width, length)
    return {
        "a1": pltpu.VMEM(wide, BF16),
        "k": pltpu.VMEM(wide, BF16),
        "v": pltpu.VMEM(wide, BF16),
        "q_t": pltpu.VMEM(tall, BF16),
        "k_t": pltpu.VMEM(tall, BF16),
        "v_t": pltpu.VMEM(tall, BF16),
        "o_t": pltpu.VMEM(tall, BF16),
        "o": pltpu.VMEM(wide, BF16),
        "g_o_t": pltpu.VMEM(tall, BF16),
        "lse": pltpu.VMEM((heads, 1, length), F32),
        "delta": pltpu.VMEM((heads, 1, length), F32),
        "x2": pltpu.VMEM(wide, F32),
        "a2": pltpu.VMEM(wide, BF16),
        "out_acc": pltpu.VMEM(wide, F32),
        "da2": pltpu.VMEM(wide, F32),
        "g_f": pltpu.VMEM(wide, BF16),
        "hr": pltpu.VMEM((length, TILE), BF16),
        "gu": pltpu.VMEM((length, TILE), BF16),
        "dk_t": pltpu.VMEM((2 * HEAD, length), F32),
        "dv_t": pltpu.VMEM((2 * HEAD, length), F32),
        "dqkv": pltpu.VMEM((length, 3 * BLOCK), BF16),
        "gvec": pltpu.VMEM((VEC_ROWS, width), F32),
        "local": pltpu.SemaphoreType.DMA((2,)),
    }


class Plain:
    def __init__(self, outs, stage, sem):
        self.outs, self.stage, self.sem = outs, stage, sem

    def begin(self):
        pass

    need_qkv = need_hidden = need_out = lambda self, *args: None

    def put(self, stage, place, make):
        stage[...] = make()
        copy = pltpu.make_async_copy(stage, place, self.sem)
        copy.start()
        copy.wait()

    def give_up(self, t, make):
        self.put(self.stage[1], self.outs[2].at[t], make)

    def give_down(self, t, make):
        self.put(self.stage[2], self.outs[3].at[t], make)

    def give_out(self, make):
        self.put(self.stage[0], self.outs[1], make)

    def give_qkv(self, j, make):
        self.put(self.stage[0], self.outs[0].at[j], make)

    def end(self):
        pass


def plain_layer(lengths, task_of, task_tokens, x, grad_out, wqkv, wout, wup, wdn, vecs):
    length, width = x.shape
    scratch = layer_scratch(length, width)
    names = tuple(scratch)

    def kernel(*refs):
        (lens, of, tokens, x, g, wqkv, wout, wup, wdn, vecs) = refs[:10]
        act, input_grad, gqkv, gout, gup, gdn, gvec = refs[10:17]
        s = Named(names, refs[17 : 17 + len(names)])
        rest = refs[17 + len(names) :]
        comm = Plain((gqkv, gout, gup, gdn), rest[:3], rest[3])
        layer_body(comm, lens, of, tokens, x, g, act, input_grad, (wqkv, wout, wup, wdn, vecs), s)
        gvec[...] = s.gvec[...]

    smem = pl.BlockSpec(memory_space=pltpu.SMEM)
    vmem = pl.BlockSpec(memory_space=pltpu.VMEM)
    hbm = pl.BlockSpec(memory_space=pl.ANY)
    like = lambda a: jax.ShapeDtypeStruct(a.shape, BF16)
    return pl.pallas_call(
        kernel,
        out_shape=(
            like(x), like(x), like(wqkv), like(wout), like(wup), like(wdn),
            jax.ShapeDtypeStruct((VEC_ROWS, width), F32),
        ),
        in_specs=[smem] * 3 + [vmem] * 7,
        out_specs=(hbm,) * 6 + (vmem,),
        scratch_shapes=list(scratch.values())
        + [
            pltpu.VMEM((width, width), BF16),
            pltpu.VMEM((width, TILE), BF16),
            pltpu.VMEM((TILE, width), BF16),
            pltpu.SemaphoreType.DMA,
        ],
        compiler_params=pltpu.CompilerParams(vmem_limit_bytes=62 * 2**20),
        name="layer",
    )(lengths, task_of, task_tokens, x, grad_out, wqkv, wout, wup, wdn, vecs)


def pack_vectors(bias_q, bias_v, bias_out, bias_up, bias_down, gain_one, shift_one, gain_two, shift_two):
    width = bias_q.shape[0]
    rows = jnp.stack([bias_q, bias_v, bias_out, bias_down, gain_one, shift_one, gain_two, shift_two])
    tiles = jnp.pad(bias_up.reshape(-1, TILE), ((0, 0), (0, width - TILE)))
    rest = jnp.zeros((VEC_ROWS - rows.shape[0] - tiles.shape[0], width), BF16)
    return jnp.concatenate([rows, tiles, rest]).astype(F32)


def plain_body(
    tokens, grad_out, lengths, task_of, task_tokens, w_qkv, w_out, w_up, w_down,
    bias_q, bias_v, bias_out, bias_up, bias_down, gain_one, shift_one, gain_two, shift_two,
):
    gather = lambda a: lax.all_gather(a, "dp", axis=0, tiled=True)
    width = tokens.shape[2]
    chunks, tiles = width // BLOCK, w_up.shape[1] // TILE
    wqkv = gather(w_qkv).reshape(width, 3, chunks, BLOCK).transpose(2, 0, 1, 3)
    wqkv = wqkv.reshape(chunks, width, 3 * BLOCK)
    wup = gather(w_up).reshape(width, tiles, TILE).transpose(1, 0, 2)
    wdn = gather(w_down).reshape(tiles, TILE, width)
    vecs = pack_vectors(
        *(gather(a) for a in (bias_q, bias_v, bias_out, bias_up, bias_down, gain_one, shift_one, gain_two, shift_two))
    )
    act, input_grad, gqkv, gout, gup, gdn, gvec = plain_layer(
        lengths, task_of, task_tokens, tokens[0], grad_out[0], wqkv, gather(w_out), wup, wdn, vecs
    )
    gqkv = gqkv.reshape(chunks, width, 3, BLOCK).transpose(1, 2, 0, 3).reshape(width, 3 * width)
    gup = gup.transpose(1, 0, 2).reshape(width, -1)
    gdn = gdn.reshape(-1, width)
    vectors = [gvec[BQ], gvec[BV], gvec[BO], gvec[UP : UP + tiles, :TILE].reshape(-1), gvec[BD]]
    vectors += [gvec[G1], gvec[S1], gvec[G2], gvec[S2]]
    grads = [gqkv, gout, gup, gdn] + [a.astype(BF16) for a in vectors]
    shares = lax.psum_scatter(grads, "dp", scatter_dimension=0, tiled=True)
    summed = jax.tree.map(lambda a: a.astype(F32), lax.psum(shares, "grp"))
    return (act[None], input_grad[None], *summed)


def solution(mesh):
    rows = P(("grp", "dp"), None, None)
    each = P(("grp", "dp"))
    matrix, vector = P("dp", None), P("dp")
    in_specs = (rows, rows, each, each, P()) + (matrix,) * 4 + (vector,) * 9
    out_specs = (rows, rows) + (matrix,) * 4 + (vector,) * 9
    body = plain_body
    return jax.shard_map(body, mesh=mesh, in_specs=in_specs, out_specs=out_specs, check_vma=False)
```

time: 599 us -> 613 us (1.023); the launches traced: 590 us -> 612 us
  matrix products: 185 us -> 0 us
  waiting for transfers between devices: 149 us -> 310 us
  Pallas kernels: 0 us -> 136 us
  other arithmetic: 84.5 us -> 8.31 us
  local copies, waits for them, and re-layouts: 79.9 us -> 69.2 us
    dot_general x96 -> x0, matrix products: 185 us -> none  [the longest x4 33 us: right_dot(): lax.dot_general(left, right, (((1,), (1,)), ((), ())), preferred_element_...]
    pallas_call x0 -> x1, Pallas kernels: none -> 136 us  [plain_layer(): pl.pallas_call(kernel, out_shape=(like(x), like(x), like(wqkv), like(wout...]
    unnamed x9 -> x11, waiting for transfers between devices: 2.66 us -> 92.1 us
    all_gather x4, waiting for transfers between devices: 0.04 us -> 72.8 us  [plain_body(): gather = lambda a: lax.all_gather(a, 'dp', axis=0, tiled=True)]
    reduce_sum x21 -> x0, other arithmetic: 27.2 us -> none  [the longest x12 13.9 us: group_forward(): lse = top + jnp.log(jnp.sum(jnp.exp(scores - top), axis=-1, keepdims=True))]
    slice x20 -> x2, local copies, waits for them, and re-layouts: 22 us -> 0.08 us  [the longest x1 0.08 us: plain_body(): vectors += [gvec[G1], gvec[S1], gvec[G2], gvec[S2]]]
    convert_element_type x35 -> x12, other arithmetic: 29.7 us -> 8.26 us  [the longest x11 7.64 us: plain_body(): summed = jax.tree.map(lambda a: a.astype(F32), lax.psum(shares, 'grp'))]
    dynamic_slice x18 -> x0, local copies, waits for them, and re-layouts: 17.7 us -> none  [one_sequence(): lax.map(lambda item: group_forward(item[0], item[1], item[2], length_s),...]
  transfers between devices with their start and end apart: 9 -> 9, of which waited for: 3 -> 8; matrix products, arithmetic and copies ran while one was open for 52% -> 10% of each run, Pallas kernels for 0% -> 0%
where the time goes in v1:
time: 613 us; the launch traced here: 612 us
  waiting for transfers between devices  310 us (51%)
  Pallas kernels  136 us (22%)
  blocking collectives  71 us (12%)
  local copies, waits for them, and re-layouts  69.2 us (11%)
  between operations  17.3 us (3%)
  other arithmetic  8.31 us (1%)
    pallas_call x1, Pallas kernels, plain_layer(): pl.pallas_call(kernel, out_shape=(like(x), like(x), like(wqkv), like(wout...  136 us
    reduce_scatter x2, waiting for transfers between devices, plain_body(): shares = lax.psum_scatter(grads, 'dp', scatter_dimension=0, tiled=True)  96.1 us
    unnamed x11, waiting for transfers between devices  92.1 us
    all_gather x4, waiting for transfers between devices, plain_body(): gather = lambda a: lax.all_gather(a, 'dp', axis=0, tiled=True)  72.8 us
    unnamed x2, blocking collectives  49.9 us
    psum x1, waiting for transfers between devices, plain_body(): summed = jax.tree.map(lambda a: a.astype(F32), lax.psum(shares, 'grp'))  48.8 us
    unnamed x39, local copies, waits for them, and re-layouts  29.9 us
    psum x1, blocking collectives, plain_body(): summed = jax.tree.map(lambda a: a.astype(F32), lax.psum(shares, 'grp'))  13.2 us
  transfers between devices with their start and end apart: 9, of which 8 were waited for; matrix products, arithmetic and copies ran while one was open for 10% of the time, Pallas kernels for 0%

profile of v1, /device:TPU:0, one launch (start us, length us, event | category | flops | bytes accessed | tf_op | source)
XLA Modules:
  0.0 611.6 jit_solution(7721262541669866392)
XLA Ops:
  10.0 1.3 fusion
  12.0 0.8 dynamic-update-slice
  14.5 0.8 dynamic-update-slice.3
  15.4 0.8 dynamic-update-slice.4
  18.7 26.0 %all-reduce.19 = (bf16[768]{0:T(1024)(128)(2,1)S(1)}, bf16[768]{0:T(1024)(128)(2,1)S(1)}, bf16[768]{0:T(1024)(128)(2,1)S(1)}, bf16[768]{0:T(1024)(128)(2,1)S(1)}...) all-reduce(bf16[768]{0:T(1024)(128)(2,1)S(1)} %dynamic-update-slice, ...), channel_id=1, replica_groups=mesh['grp'=4,'dp'=8] {'dp'}, use_global_device_ids=true, to_apply=%add.1 | all-reduce | flops 6144 | bytes 24576
  45.5 7.9 %all-gather = bf16[8,1,384]{2,1,0:T(2,128)(2,1)S(1)} all-gather(bf16[1,1,384]{2,1,0:T(2,128)(2,1)S(1)} %reshape.100), channel_id=1, replica_groups=mesh['grp'=4,'dp'=8] {'dp'}, dimensions={0}, use_global_device_ids=true | all-gather | bytes 6912 | tf_op jit(solution)/shard_map/all_gather | solution.py:458
  55.6 4.6 copy.55
  60.2 2.0 copy.56
  62.2 6.0 copy.59.refs_5_
  68.2 19.4 %all-gather.10.cloned.1.call-done = bf16[768,3072]{1,0:T(8,128)(2,1)} async-done(((bf16[96,3072]{1,0:T(8,128)(2,1)}), bf16[768,3072]{1,0:T(8,128)(2,1)}) %all-gather.10.cloned.1.call-update) | async-done | bytes 4718608 | tf_op jit(solution)/shard_map/all_gather | solution.py:458
  87.7 6.6 %copy.57 = bf16[768,3072]{0,1:T(8,128)(2,1)} copy(bf16[768,3072]{1,0:T(8,128)(2,1)} %all-gather.10.cloned.1.call-done) | data formatting | bytes 9437184 | tf_op jit(solution)/shard_map/all_gather | solution.py:458
  94.3 6.7 %copy.58 = bf16[768,6,512]{2,0,1:T(8,128)(2,1)} copy(bf16[768,6,512]{0,2,1:T(8,128)(2,1)} %bitcast.22) | data formatting | bytes 9437184 | tf_op jit(solution)/shard_map/reshape | solution.py:463
  101.0 12.6 %all-gather.8.cloned.1.call-done.refs_6_ = bf16[768,768]{1,0:T(8,128)(2,1)} async-done(((bf16[96,768]{1,0:T(8,128)(2,1)}), bf16[768,768]{1,0:T(8,128)(2,1)}) %all-gather.8.cloned.1.call-update) | async-done | bytes 1179664 | tf_op jit(solution)/shard_map/all_gather | solution.py:458
  113.7 40.7 %all-gather.12.cloned.1.call-done = bf16[3072,768]{1,0:T(8,128)(2,1)} async-done(((bf16[384,768]{1,0:T(8,128)(2,1)}), bf16[3072,768]{1,0:T(8,128)(2,1)}) %all-gather.12.cloned.1.call-update) | async-done | bytes 4718608 | tf_op jit(solution)/shard_map/all_gather | solution.py:458
  154.3 135.6 %layer.1 = (bf16[1024,768]{1,0:T(8,128)(2,1)}, bf16[1024,768]{1,0:T(8,128)(2,1)}, bf16[3,768,768]{2,1,0:T(8,128)(2,1)}, bf16[768,768]{1,0:T(8,128)(2,1)}, bf16[6...) custom-call(s32[1]{0:T(128)S(6)} %copy.82.refs_0_, s32[1]{0:T(128)S(6)} %copy.83.refs_1_, ...), custom_call_target="tpu_custom_call" | custom-call | tf_op jit(solution)/shard_map/layer/pallas_call | solution.py:426
  290.0 4.3 copy.60
  294.3 2.0 copy.61
  296.3 5.8 copy.65
  302.1 6.7 %copy.62 = bf16[768,6,512]{0,2,1:T(8,128)(2,1)} copy(bf16[768,6,512]{2,0,1:T(8,128)(2,1)} %bitcast.30) | data formatting | bytes 9437184 | tf_op jit(solution)/shard_map/transpose | solution.py:472
  308.9 6.9 %copy.67 = bf16[768,3072]{1,0:T(8,128)(2,1)} copy(bf16[768,3072]{0,1:T(8,128)(2,1)} %bitcast.23) | data formatting | bytes 9437184
  317.3 33.0 %reduce-scatter.13.cloned.1.call-done = bf16[96,2304]{1,0:T(8,128)(2,1)} async-done(((bf16[768,2304]{1,0:T(8,128)(2,1)}), bf16[96,2304]{1,0:T(8,128)(2,1)}) %reduce-scatter.13.cloned.1.call-update) | async-done | bytes 442384
  350.3 2.1 copy.66
  352.4 55.1 %reduce-scatter.15.cloned.1.call-done = bf16[96,3072]{1,0:T(8,128)(2,1)} async-done(((bf16[768,3072]{1,0:T(8,128)(2,1)}), bf16[96,3072]{1,0:T(8,128)(2,1)}) %reduce-scatter.15.cloned.1.call-update) | async-done | bytes 589840
  407.5 2.2 copy.68
  409.7 38.7 %reduce-scatter.9.cloned.1.call-done = bf16[96,768]{1,0:T(8,128)(2,1)} async-done(((bf16[768,768]{1,0:T(8,128)(2,1)}), bf16[96,768]{1,0:T(8,128)(2,1)}) %reduce-scatter.9.cloned.1.call-update) | async-done | bytes 147472 | tf_op jit(solution)/shard_map/reduce_scatter | solution.py:477
  448.5 57.3 %reduce-scatter.11.cloned.1.call-done = bf16[384,768]{1,0:T(8,128)(2,1)} async-done(((bf16[3072,768]{1,0:T(8,128)(2,1)}), bf16[384,768]{1,0:T(8,128)(2,1)}) %reduce-scatter.11.cloned.1.call-update) | async-done | bytes 589840 | tf_op jit(solution)/shard_map/reduce_scatter | solution.py:477
  507.3 23.9 %all-reduce.18 = (bf16[768]{0:T(1024)(128)(2,1)S(1)}, bf16[768]{0:T(1024)(128)(2,1)S(1)}, bf16[768]{0:T(1024)(128)(2,1)S(1)}, bf16[3072]{0:T(1024)(128)(2,1)S(1)...) all-reduce(bf16[768]{0:T(1024)(128)(2,1)S(1)} %get-tuple-element.81, ...), channel_id=6, replica_groups=mesh['grp'=4,'dp'=8] {'dp'}, use_global_device_ids=true, to_apply=%region_8.9.clone | all-reduce | flops 9216 | bytes 36864
  531.9 13.2 %all-reduce.20 = (bf16[96]{0:T(256)(128)(2,1)S(1)}, bf16[96]{0:T(256)(128)(2,1)S(1)}, bf16[96]{0:T(256)(128)(2,1)S(1)}, bf16[384]{0:T(512)(128)(2,1)S(1)}, bf16[...) all-reduce(bf16[96]{0:T(256)(128)(2,1)S(1)} %dynamic-slice.9, ...), channel_id=1, replica_groups=mesh['grp'=4,'dp'=8] {'grp'}, use_global_device_ids=true, to_apply=%region_9.10 | all-reduce | flops 1152 | bytes 4608 | tf_op jit(solution)/shard_map/psum | solution.py:478
  549.7 48.8 %all-reduce.24.cloned.1.call-done = (bf16[96,2304]{0,1:T(8,128)(2,1)}, bf16[96,3072]{0,1:T(8,128)(2,1)}, bf16[96,768]{1,0:T(8,128)(2,1)}, bf16[384,768]{1,0:T(8,128)(2,1)}) async-done(((bf16[96,2304]{0,1:T(8,128)(2,1)}, bf16[96,3072]{0,1:T(8,128)(2,1)}, bf16[96,768]{1,0:T(8,128)(2,1)}, bf16[384,768]{1,0:T(8,128)(2,1)}), (bf16[96,2304]{0,1:T(8,128)(2,1)}, bf16[96,3072]{0,1:T(8,128)(2,1)}, ...) | async-done | bytes 1769488 | tf_op jit(solution)/shard_map/psum | solution.py:478
  598.5 2.2 convert_element_type.84
  600.8 2.4 copy.64
  603.2 1.2 copy.63
  (76 shorter events, 16.3 us)
Async XLA Ops:
  7.2 48.4 %all-gather.6.cloned.1.call-start = ((), (), s32[]{:S(2)}) async-start(), calls=%async_computation.4 | async-start | bytes 3981312 | tf_op jit(solution)/shard_map/all_gather | solution.py:458
  7.9 79.8 %all-gather.10.cloned.1.call-start = ((), (), s32[]{:S(2)}) async-start(), calls=%async_computation.6 | async-start | bytes 5308416 | tf_op jit(solution)/shard_map/all_gather | solution.py:458
  8.7 105.0 %all-gather.8.cloned.1.call-start = ((), (), s32[]{:S(2)}) async-start(), calls=%async_computation.5 | async-start | bytes 1327104 | tf_op jit(solution)/shard_map/all_gather | solution.py:458
  9.4 144.9 %all-gather.12.cloned.1.call-start = ((), (), s32[]{:S(2)}) async-start(), calls=%async_computation.7 | async-start | bytes 5308416 | tf_op jit(solution)/shard_map/all_gather | solution.py:458
  10.0 340.3 %reduce-scatter.13.cloned.1.call-start = ((), (), s32[]{:S(2)}) async-start(), calls=%async_computation.10 | async-start | bytes 3981312
  302.1 105.4 %reduce-scatter.15.cloned.1.call-start = ((), (), s32[]{:S(2)}) async-start(), calls=%async_computation.11 | async-start | bytes 5308416
  315.8 132.7 %reduce-scatter.9.cloned.1.call-start = ((), (), s32[]{:S(2)}) async-start(), calls=%async_computation.8 | async-start | bytes 1327104 | tf_op jit(solution)/shard_map/reduce_scatter | solution.py:477
  316.5 189.3 %reduce-scatter.11.cloned.1.call-start = ((), (), s32[]{:S(2)}) async-start(), calls=%async_computation.9 | async-start | bytes 5308416 | tf_op jit(solution)/shard_map/reduce_scatter | solution.py:477
  316.6 190.6 %copy-start.2 = (f32[16,768]{1,0:T(8,128)S(1)}, f32[16,768]{1,0:T(8,128)}, u32[]{:S(2)}) copy-start(f32[16,768]{1,0:T(8,128)} %get-tuple-element.28) | copy-start | bytes 147460
  317.3 281.3 %all-reduce.24.cloned.1.call-start = ((), (), s32[]{:S(2)}) async-start(), calls=%async_computation.12 | async-start | bytes 4227072 | tf_op jit(solution)/shard_map/psum | solution.py:478
  598.5 4.6 copy-start
  598.5 5.8 copy-start.1
Sparse Core Ops, SparseCore 0:
  9.9 36.8 all-gather.5
  48.7 38.9 all-gather.9
  89.6 24.0 all-gather.7
  115.4 38.9 all-gather.11
  302.2 48.0 reduce-scatter.12
  353.6 53.8 reduce-scatter.14
  411.6 36.7 reduce-scatter.8
  451.9 53.8 reduce-scatter.10
  509.2 89.2 all-reduce.23

commit v2 on v1

--- a/solution.py
+++ b/solution.py
@@ -58,12 +58,14 @@
     return pl.ds(pl.multiple_of(index * size, size), size)
 
 
-def norm_one_phase(x, vecs, a1):
+def norm_one_phase(x, vecs, a1, x2):
     gain, shift = vecs[G1 : G1 + 1, :], vecs[S1 : S1 + 1, :]
 
     def step(i, _):
         at = rows_at(i)
-        normed, _ = norm_rows(x[at, :].astype(F32))
+        value = x[at, :].astype(F32)
+        x2[at, :] = value
+        normed, _ = norm_rows(value)
         a1[at, :] = (normed * gain + shift).astype(BF16)
         return 0
 
@@ -89,7 +91,7 @@
     return jnp.concatenate([rows, zeros] if side == 0 else [zeros, rows], axis=0)
 
 
-def attend_pair(p, length_s, k, q_t, v_t, o_t, o, lse):
+def attend_pair(p, length_s, k, q_t, v_t, o_t, lse):
     length = k.shape[0]
     lanes = rows_at(p, 2 * HEAD)
     for i in range(length // BLOCK):
@@ -111,9 +113,7 @@
             lse[head, :, cols] = jnp.where(queries < length_s, top + jnp.log(total), 1e30)
             result = nn(v_t[at, :seen], weights.astype(BF16)) * (1.0 / total)
             halves.append(result.astype(BF16))
-        both = jnp.concatenate(halves, axis=0)
-        o_t[lanes, cols] = both
-        o[cols, lanes] = both.T
+        o_t[lanes, cols] = jnp.concatenate(halves, axis=0)
 
 
 def attend_back_pair(p, k, v, q_t, k_t, g_o_t, lse, delta, dk_t, dv_t, dqkv, gvec):
@@ -162,20 +162,17 @@
     gvec[BV : BV + 1, lanes] = column_sum(dv.astype(F32))
 
 
-def norm_two_phase(x, o, wout, vecs, x2, a2, out_acc):
+def norm_two_phase(o_t, wout, vecs, x2, a2, out_acc):
     bias, down = vecs[BO : BO + 1, :], vecs[BD : BD + 1, :]
     gain, shift = vecs[G2 : G2 + 1, :], vecs[S2 : S2 + 1, :]
 
-    def step(i, _):
-        at = rows_at(i)
-        value = x[at, :].astype(F32) + nn(o[at, :], wout[...]) + bias
+    for i in range(x2.shape[0] // BLOCK):
+        at = slice(i * BLOCK, (i + 1) * BLOCK)
+        value = x2[at, :] + tn(o_t[:, at], wout[...]) + bias
         x2[at, :] = value
         out_acc[at, :] = value + down
         normed, _ = norm_rows(value)
         a2[at, :] = (normed * gain + shift).astype(BF16)
-        return 0
-
-    lax.fori_loop(0, x.shape[0] // BLOCK, step, 0)
 
 
 def cotangent_rows(i, grad_out, length_s, weight_s):
@@ -279,7 +276,7 @@
     s.gvec[...] = jnp.zeros_like(s.gvec)
     s.da2[...] = jnp.zeros_like(s.da2)
     comm.begin()
-    norm_one_phase(x, vecs, s.a1)
+    norm_one_phase(x, vecs, s.a1, s.x2)
     branch_phase(grad_out, length_s, weight_s, s.g_f, s.gvec)
 
     def forward(j, _):
@@ -287,20 +284,23 @@
         qkv_phase(j, s.a1, wqkv, vecs, s.k, s.v, s.q_t, s.k_t, s.v_t)
 
         def pair(p, _):
-            attend_pair(2 * j + p, length_s, s.k, s.q_t, s.v_t, s.o_t, s.o, s.lse)
+            attend_pair(2 * j + p, length_s, s.k, s.q_t, s.v_t, s.o_t, s.lse)
             return 0
 
         return lax.fori_loop(0, 2, pair, 0)
 
     lax.fori_loop(0, wqkv.shape[0], forward, 0)
     comm.need_out()
-    norm_two_phase(x, s.o, wout, vecs, s.x2, s.a2, s.out_acc)
+    norm_two_phase(s.o_t, wout, vecs, s.x2, s.a2, s.out_acc)
+
+    hr, gu, dqkv = s.work.at[:, :TILE], s.work.at[:, TILE:], s.work.at[:, : 3 * BLOCK]
+    g_o_t = s.v_t
 
     def hidden(t, _):
         comm.need_hidden(t)
-        hidden_tile(t, s.a2, s.g_f, wup, wdn, vecs, s.out_acc, s.da2, s.hr, s.gu, s.gvec)
-        comm.give_up(t, lambda: tn(s.a2[...], s.gu[...]).astype(BF16))
-        comm.give_down(t, lambda: tn(s.hr[...], s.g_f[...]).astype(BF16))
+        hidden_tile(t, s.a2, s.g_f, wup, wdn, vecs, s.out_acc, s.da2, hr, gu, s.gvec)
+        comm.give_up(t, lambda: tn(s.a2[...], gu[...]).astype(BF16))
+        comm.give_down(t, lambda: tn(hr[...], s.g_f[...]).astype(BF16))
         return 0
 
     lax.fori_loop(0, wup.shape[0], hidden, 0)
@@ -309,24 +309,24 @@
     )
     act_copy = pltpu.make_async_copy(s.g_f, act, s.local.at[0])
     act_copy.start()
-    comm.give_out(lambda: tn(s.o[...], s.a2[...]).astype(BF16))
-    attended_back(wout, s.a2, s.o_t, s.g_o_t, s.delta)
+    comm.give_out(lambda: nn(s.o_t[...], s.a2[...]).astype(BF16))
+    attended_back(wout, s.a2, s.o_t, g_o_t, s.delta)
     da1 = s.out_acc
     da1[...] = jnp.zeros_like(da1)
 
     def backward(j, _):
         def pair(p, _):
             attend_back_pair(
-                2 * j + p, s.k, s.v, s.q_t, s.k_t, s.g_o_t, s.lse, s.delta,
-                s.dk_t, s.dv_t, s.dqkv, s.gvec,
+                2 * j + p, s.k, s.v, s.q_t, s.k_t, g_o_t, s.lse, s.delta,
+                s.dk_t, s.dv_t, dqkv, s.gvec,
             )
             return 0
 
         lax.fori_loop(0, 2, pair, 0)
-        comm.give_qkv(j, lambda: tn(s.a1[...], s.dqkv[...]).astype(BF16))
+        comm.give_qkv(j, lambda: tn(s.a1[...], dqkv[...]).astype(BF16))
         for m in range(x.shape[0] // BLOCK):
             at = slice(m * BLOCK, (m + 1) * BLOCK)
-            da1[at, :] += nt(s.dqkv[at, :], wqkv[j])
+            da1[at, :] += nt(dqkv[at, :], wqkv[j])
         return 0
 
     lax.fori_loop(0, wqkv.shape[0], backward, 0)
@@ -355,8 +355,6 @@
         "k_t": pltpu.VMEM(tall, BF16),
         "v_t": pltpu.VMEM(tall, BF16),
         "o_t": pltpu.VMEM(tall, BF16),
-        "o": pltpu.VMEM(wide, BF16),
-        "g_o_t": pltpu.VMEM(tall, BF16),
         "lse": pltpu.VMEM((heads, 1, length), F32),
         "delta": pltpu.VMEM((heads, 1, length), F32),
         "x2": pltpu.VMEM(wide, F32),
@@ -364,11 +362,9 @@
         "out_acc": pltpu.VMEM(wide, F32),
         "da2": pltpu.VMEM(wide, F32),
         "g_f": pltpu.VMEM(wide, BF16),
-        "hr": pltpu.VMEM((length, TILE), BF16),
-        "gu": pltpu.VMEM((length, TILE), BF16),
+        "work": pltpu.VMEM((length, 2 * TILE), BF16),
         "dk_t": pltpu.VMEM((2 * HEAD, length), F32),
         "dv_t": pltpu.VMEM((2 * HEAD, length), F32),
-        "dqkv": pltpu.VMEM((length, 3 * BLOCK), BF16),
         "gvec": pltpu.VMEM((VEC_ROWS, width), F32),
         "local": pltpu.SemaphoreType.DMA((2,)),
     }
@@ -479,11 +475,667 @@
     return (act[None], input_grad[None], *summed)
 
 
+MESH = pl.DeviceIdType.MESH
+
+
+class Place:
+    def __init__(self):
+        z, d = lax.axis_index("grp"), lax.axis_index("dp")
+        self.z, self.d = z, d
+        self.core = lax.rem(d, 2)
+        self.chip = d // 2
+        x, y = lax.rem(self.chip, 2), d // 4
+        self.d_core = d + 1 - 2 * self.core
+        self.d_x = d + 2 - 4 * x
+        self.d_y = d + 4 - 8 * y
+        self.d_diag = self.d_x + 4 - 8 * y
+        self.chip_x, self.chip_y, self.chip_diag = self.d_x // 2, self.d_y // 2, self.d_diag // 2
+        self.on_core, self.on_x, self.on_y = ((z, e) for e in (self.d_core, self.d_x, self.d_y))
+        self.outer = (z == 0) | (z == 3)
+        self.inner = (z == 1) | (z == 2)
+        self.to_inner = (1 + z // 3, d)
+        self.to_outer = (3 * (z // 2), d)
+        self.to_mid = (3 - z, d)
+
+
+def remote(src, dst, sems, index, device):
+    send, recv = sems
+    return pltpu.make_async_remote_copy(
+        src_ref=src, dst_ref=dst, send_sem=send.at[index], recv_sem=recv.at[index],
+        device_id=device, device_id_type=MESH,
+    )
+
+
+class Gather:
+    def __init__(self, here, full, sems):
+        self.here, self.full, self.sems = here, full, sems
+        self.count, rows, _ = full.shape
+        self.rows = rows // 8
+
+    def block(self, i, owner, half=None):
+        rows = self.rows if half is None else self.rows // 2
+        start = owner * self.rows + (0 if half is None else half * rows)
+        return self.full.at[i, pl.ds(pl.multiple_of(start, 16), rows), :]
+
+    def copy(self, i, n):
+        p = self.here
+        owner, half, device = (
+            (p.d, None, p.on_x),
+            (p.d, None, p.on_y),
+            (p.d, None, p.on_core),
+            (p.d_x, None, p.on_core),
+            (p.d_x, 0, p.on_y),
+            (p.d_y, None, p.on_core),
+            (p.d_y, 1, p.on_x),
+            (p.d_diag, None, p.on_core),
+        )[n]
+        part = self.block(i, owner, half)
+        return remote(part, part, self.sems, (n, i), device)
+
+    def landed(self, i, n):
+        p = self.here
+        flip = 1 - 2 * p.core
+        owner, half = (
+            (p.d_x, None),
+            (p.d_y, None),
+            (p.d_core, None),
+            (p.d_x + flip, None),
+            (p.d_diag, 0),
+            (p.d_y + flip, None),
+            (p.d_diag, 1),
+            (p.d_diag + flip, None),
+        )[n]
+        part = self.block(i, owner, half)
+        remote(part, part, self.sems, (n, i), p.on_core).wait_recv()
+
+    def start(self, i):
+        for n in (0, 1, 2):
+            self.copy(i, n).start()
+
+    def relay(self, i):
+        self.landed(i, 0)
+        self.copy(i, 4).start()
+        self.copy(i, 3).start()
+        self.landed(i, 1)
+        self.copy(i, 6).start()
+        self.copy(i, 5).start()
+
+    def diag(self, i):
+        self.landed(i, 4)
+        self.landed(i, 6)
+        self.copy(i, 7).start()
+
+    def need(self, i):
+        for n in (2, 3, 5, 7):
+            self.landed(i, n)
+
+    def drain(self):
+        def step(i, _):
+            for n in range(8):
+                self.copy(i, n).wait_send()
+            return 0
+
+        lax.fori_loop(0, self.count, step, 0)
+
+
+def added(*refs_at):
+    total = refs_at[0].astype(F32)
+    for value in refs_at[1:]:
+        total = total + value.astype(F32)
+    return total.astype(BF16)
+
+
+class Reduce:
+    STAGES = 7
+
+    def __init__(self, here, bufs, sems):
+        self.here, self.sems = here, sems
+        (self.sums, self.from_core, self.half_x, self.half_y, self.from_x, self.from_y,
+         self.run, self.from_outer, self.from_mid, self.total) = bufs
+        self.count, self.rows, self.columns = self.total.shape
+        self.slots, self.run_slots = self.sums.shape[0] - 1, self.run.shape[0]
+        self.outer_slots = self.from_outer.shape[0]
+
+    @staticmethod
+    def buffers(count, rows, columns, slots, run_slots):
+        piece = (rows, columns)
+        shapes = [(slots + 1, 4) + piece, (2, 4) + piece]
+        shapes += [(2, rows // 2, columns)] * 2 + [(2,) + piece] * 2
+        shapes += [(run_slots,) + piece, (run_slots,) + piece, (2,) + piece, (count,) + piece]
+        return [pltpu.VMEM(shape, BF16) for shape in shapes]
+
+    def mine(self, i):
+        return 1 + lax.rem(i, self.slots)
+
+    def copy(self, i, n):
+        p, two, half = self.here, lax.rem(i, 2), self.rows // 2
+        own = self.mine(i)
+        run = self.run.at[lax.rem(i, self.run_slots)]
+        src, dst, device = (
+            lambda: (self.sums.at[0], self.from_core.at[two], p.on_core),
+            lambda: (self.sums.at[own, p.chip_diag, :half], self.half_x.at[two], p.on_x),
+            lambda: (self.sums.at[own, p.chip_diag, half:], self.half_y.at[two], p.on_y),
+            lambda: (self.sums.at[own, p.chip_x], self.from_x.at[two], p.on_x),
+            lambda: (self.sums.at[own, p.chip_y], self.from_y.at[two], p.on_y),
+            lambda: (run, self.from_outer.at[lax.rem(i, self.outer_slots)], p.to_inner),
+            lambda: (run, self.from_mid.at[two], p.to_mid),
+            lambda: (self.total.at[i], self.total.at[i], p.to_outer),
+        )[n]()
+        return remote(src, dst, self.sems, (n, i), device)
+
+    def stage_0(self, i, value):
+        own, rows = self.mine(i), self.rows
+        for owner in range(8):
+            same = 1 - lax.rem(self.here.core + owner, 2)
+            self.sums[same * own, owner // 2] = value[owner * rows : (owner + 1) * rows]
+        self.copy(i, 0).start()
+
+    def stage_1(self, i):
+        own, two = self.mine(i), lax.rem(i, 2)
+        done = self.copy(i, 0)
+        done.wait_recv()
+        done.wait_send()
+        order = (self.here.chip_diag, self.here.chip_x, self.here.chip_y, self.here.chip)
+        for n, chip in enumerate(order):
+            self.sums[own, chip] = added(self.sums[own, chip], self.from_core[two, chip])
+            if n == 0:
+                self.copy(i, 1).start()
+                self.copy(i, 2).start()
+
+    def stage_2(self, i):
+        p, own, two, half = self.here, self.mine(i), lax.rem(i, 2), self.rows // 2
+        self.copy(i, 1).wait_recv()
+        self.sums[own, p.chip_y, :half] = added(self.sums[own, p.chip_y, :half], self.half_x[two])
+        self.copy(i, 4).start()
+        self.copy(i, 2).wait_recv()
+        self.sums[own, p.chip_x, half:] = added(self.sums[own, p.chip_x, half:], self.half_y[two])
+        self.copy(i, 3).start()
+
+    def stage_3(self, i):
+        p, own, two = self.here, self.mine(i), lax.rem(i, 2)
+        self.copy(i, 3).wait_recv()
+        self.copy(i, 4).wait_recv()
+        self.run[lax.rem(i, self.run_slots)] = added(
+            self.sums[own, p.chip], self.from_x[two], self.from_y[two]
+        )
+        for n in (1, 2, 3, 4):
+            self.copy(i, n).wait_send()
+        pl.when(p.outer)(lambda: self.copy(i, 5).start())
+
+    def stage_4(self, i):
+        def work():
+            self.copy(i, 5).wait_recv()
+            at = lax.rem(i, self.run_slots)
+            self.run[at] = added(self.run[at], self.from_outer[lax.rem(i, self.outer_slots)])
+            self.copy(i, 6).start()
+
+        pl.when(self.here.inner)(work)
+
+    def stage_5(self, i):
+        def work():
+            self.copy(i, 6).wait_recv()
+            self.total[i] = added(self.run[lax.rem(i, self.run_slots)], self.from_mid[lax.rem(i, 2)])
+            self.copy(i, 7).start()
+
+        pl.when(self.here.inner)(work)
+
+    def stage_6(self, i):
+        def finish_inner():
+            self.copy(i, 6).wait_send()
+            self.copy(i, 7).wait_send()
+
+        def finish_outer():
+            self.copy(i, 5).wait_send()
+            self.copy(i, 7).wait_recv()
+
+        pl.when(self.here.inner)(finish_inner)
+        pl.when(self.here.outer)(finish_outer)
+
+    def stage(self, s, i):
+        getattr(self, "stage_%d" % s)(i)
+
+    def guarded(self, s, i):
+        pl.when((i >= 0) & (i < self.count))(lambda: self.stage(s, i))
+
+
+class Fused:
+    def __init__(self, here, ins, outs, g, c):
+        self.here, self.ins, self.outs, self.g, self.c = here, ins, outs, g, c
+        self.gather = {
+            kind: Gather(here, g[kind], (c["g_send_" + kind], c["g_recv_" + kind])) for kind in "qud"
+        }
+        self.reduce = {
+            kind: Reduce(here, c["r_" + kind], (c["r_send_" + kind], c["r_recv_" + kind]))
+            for kind in "qud"
+        }
+
+    def greet(self):
+        p, barrier = self.here, pltpu.get_barrier_semaphore()
+        for step in range(1, 8):
+            pl.semaphore_signal(
+                barrier, inc=1, device_id=(p.z, lax.rem(p.d + step, 8)), device_id_type=MESH
+            )
+        for step in range(1, 4):
+            pl.semaphore_signal(
+                barrier, inc=1, device_id=(lax.rem(p.z + step, 4), p.d), device_id_type=MESH
+            )
+        pl.semaphore_wait(barrier, 10)
+
+    def vector_copy(self, kind, step):
+        p, c = self.here, self.c
+        sems = (c["v_send"], c["v_recv"])
+        if kind == 2:
+            device = (lax.rem(p.z + step, 4), p.d)
+            return remote(c["vz"].at[p.z], c["vz"].at[p.z], sems, (kind, step), device)
+        device = (p.z, lax.rem(p.d + step, 8))
+        if kind == 0:
+            return remote(self.ins["vec"], c["vfull"].at[p.d], sems, (kind, step), device)
+        return remote(c["vpack"].at[device[1]], c["vin"].at[step], sems, (kind, step), device)
+
+    def vector_landed(self, kind, step):
+        p, c = self.here, self.c
+        sems = (c["v_send"], c["v_recv"])
+        if kind == 2:
+            part = c["vz"].at[lax.rem(p.z + 4 - step, 4)]
+        elif kind == 0:
+            part = c["vfull"].at[lax.rem(p.d + 8 - step, 8)]
+        else:
+            part = c["vin"].at[step]
+        remote(part, part, sems, (kind, step), p.on_core).wait_recv()
+
+    def own_copies(self):
+        p, ins, g, sem = self.here, self.ins, self.g, self.c["own"]
+        rows, width = ins["out"].shape
+        parts = [[], [], [], [], []]
+        at = pl.ds(pl.multiple_of(p.d * rows, 16), rows)
+        for j in range(3):
+            for part in range(3):
+                src = ins["qkv"].at[:, pl.ds(part * width + j * BLOCK, BLOCK)]
+                parts[j].append((src, g["q"].at[j, at, pl.ds(part * BLOCK, BLOCK)]))
+        parts[3].append((ins["out"], g["q"].at[3, at, :]))
+        for t in range(6):
+            down = pl.ds(pl.multiple_of(p.d * 64, 16), 64)
+            parts[4].append((ins["down"].at[pl.ds(64 * t, 64), :], g["d"].at[t, down, :]))
+        copies = []
+        for n, part in enumerate(parts):
+            copies.append([pltpu.make_async_copy(src, dst, sem.at[n]) for src, dst in part])
+        return copies
+
+    def up_copies(self, room):
+        rows = self.ins["up"].shape[0]
+        return [
+            pltpu.make_async_copy(
+                self.ins["up"].at[:, pl.ds(1024 * b, 1024)],
+                room.at[pl.ds(rows * b, rows), :],
+                self.c["own"].at[5],
+            )
+            for b in range(3)
+        ]
+
+    def place_up(self, room):
+        rows = self.ins["up"].shape[0]
+        at = pl.ds(pl.multiple_of(self.here.d * rows, 16), rows)
+
+        def piece(owner, t):
+            start = 384 * owner + 64 * t
+            block, off = start // 1024, start % 1024
+            return room[block * rows : (block + 1) * rows, off : off + 64]
+
+        for t in range(6):
+            for pair in range(4):
+                both = jnp.concatenate([piece(2 * pair, t), piece(2 * pair + 1, t)], axis=1)
+                self.g["u"][t, at, 128 * pair : 128 * (pair + 1)] = both
+
+    def spread_vectors(self, vecs):
+        vfull = self.c["vfull"]
+        vecs[...] = jnp.zeros_like(vecs)
+        rows = self.ins["out"].shape[0]
+        for owner in range(8):
+            vecs[0:8, rows * owner : rows * (owner + 1)] = vfull[owner, 0:8, :rows]
+            vecs[8:14, 64 * owner : 64 * (owner + 1)] = vfull[owner, 8:14, :64]
+
+    def pack_vectors(self, gvec):
+        vpack = self.c["vpack"]
+        vpack[...] = jnp.zeros_like(vpack)
+        rows = self.ins["out"].shape[0]
+        for owner in range(8):
+            vpack[owner, 0:8, :rows] = gvec[0:8, rows * owner : rows * (owner + 1)]
+            vpack[owner, 8:14, :64] = gvec[8:14, 64 * owner : 64 * (owner + 1)]
+
+
+def fused_body(comm, lengths, task_of, task_tokens, hbm_x, hbm_grad, act, input_grad, vecs, s):
+    here, c, g = comm.here, comm.c, comm.g
+    gq, gu, gd = (comm.gather[kind] for kind in "qud")
+    rq, ru, rd = (comm.reduce[kind] for kind in "qud")
+    wq, wup, wdn = g["q"], g["u"], g["d"]
+    wout = wq.at[3]
+    length_s = lengths[0]
+    weight_s = task_weight(task_of, task_tokens)
+    get_x = pltpu.make_async_copy(hbm_x, s.x, s.local.at[2])
+    get_grad = pltpu.make_async_copy(hbm_grad, s.x, s.local.at[3])
+    get_x_again = pltpu.make_async_copy(hbm_x, s.x, s.local.at[4])
+    own = comm.own_copies()
+    ups = comm.up_copies(s.o_t)
+    own_vec = pltpu.make_async_copy(comm.ins["vec"], c["vfull"].at[here.d], c["own"].at[6])
+    for copy in own[0] + [own_vec] + own[1] + own[2] + [get_x] + ups + own[3] + own[4]:
+        copy.start()
+    s.gvec[...] = jnp.zeros_like(s.gvec)
+    s.da2[...] = jnp.zeros_like(s.da2)
+    comm.greet()
+    for step in range(1, 8):
+        comm.vector_copy(0, step).start()
+    for j in range(2):
+        for copy in own[j]:
+            copy.wait()
+        gq.start(j)
+    for copy in ups:
+        copy.wait()
+    comm.place_up(s.o_t)
+    own_vec.wait()
+    for step in range(1, 8):
+        comm.vector_landed(0, step)
+    comm.spread_vectors(vecs)
+    get_x.wait()
+    norm_one_phase(s.x, vecs, s.a1, s.x2)
+    get_grad.start()
+    gq.relay(0)
+    for copy in own[2] + own[3] + own[4]:
+        copy.wait()
+    gq.diag(0)
+
+    def hidden_start(t):
+        gu.start(t)
+        gd.start(t)
+
+    def hidden_relay(t):
+        gu.relay(t)
+        gd.relay(t)
+
+    def hidden_diag(t):
+        gu.diag(t)
+        gd.diag(t)
+
+    def forward(j, _):
+        pl.when(j < 2)(lambda: gq.start(j + 2))
+        pl.when(j == 2)(lambda: hidden_start(0))
+        gq.need(j)
+        qkv_phase(j, s.a1, wq, vecs, s.k, s.v, s.q_t, s.k_t, s.v_t)
+        gq.relay(j + 1)
+
+        def pair(n, _):
+            attend_pair(2 * j + n, length_s, s.k, s.q_t, s.v_t, s.o_t, s.lse)
+            pl.when(n == 0)(lambda: gq.diag(j + 1))
+            return 0
+
+        return lax.fori_loop(0, 2, pair, 0)
+
+    lax.fori_loop(0, 3, forward, 0)
+    hidden_start(1)
+    hidden_relay(0)
+    get_grad.wait()
+    branch_phase(s.x, length_s, weight_s, s.g_f, s.gvec)
+    gq.need(3)
+    norm_two_phase(s.o_t, wout, vecs, s.x2, s.a2, s.out_acc)
+    hidden_diag(0)
+    hr, gu_tile = s.work.at[:, :TILE], s.work.at[:, TILE:]
+
+    def hidden(t, _):
+        pl.when(t < 4)(lambda: hidden_start(t + 2))
+        gu.need(t)
+        gd.need(t)
+        hidden_tile(t, s.a2, s.g_f, wup, wdn, vecs, s.out_acc, s.da2, hr, gu_tile, s.gvec)
+        pl.when(t < 5)(lambda: hidden_relay(t + 1))
+        for stage in range(6, 0, -1):
+            ru.guarded(stage, t - stage)
+            rd.guarded(stage, t - stage)
+        ru.stage_0(t, tn(s.a2[...], gu_tile[...]).astype(BF16))
+        rd.stage_0(t, tn(hr[...], s.g_f[...]).astype(BF16))
+        pl.when(t < 5)(lambda: hidden_diag(t + 1))
+        return 0
+
+    lax.fori_loop(0, 6, hidden, 0)
+
+    def hidden_point(step):
+        for stage in range(6, 0, -1):
+            item = step - stage
+            if isinstance(step, int):
+                if 0 <= item < 6:
+                    ru.stage(stage, item)
+                    rd.stage(stage, item)
+            else:
+                ru.guarded(stage, item)
+                rd.guarded(stage, item)
+
+    norm_two_back(s.x, length_s, weight_s, s.x2, s.da2, vecs, s.a2, s.gvec, s.out_acc, s.g_f)
+    get_x_again.start()
+    act_copy = pltpu.make_async_copy(s.g_f, act, s.local.at[0])
+    act_copy.start()
+    hidden_point(6)
+    rq.stage_0(0, nn(s.o_t[...], s.a2[...]).astype(BF16))
+    g_o_t = s.v_t
+    attended_back(wout, s.a2, s.o_t, g_o_t, s.delta)
+    hidden_point(7)
+    da1 = s.out_acc
+    da1[...] = jnp.zeros_like(da1)
+    dqkv = s.work.at[:, : 3 * BLOCK]
+
+    def backward(j, _):
+        def pair(n, _):
+            attend_back_pair(
+                2 * j + n, s.k, s.v, s.q_t, s.k_t, g_o_t, s.lse, s.delta,
+                s.dk_t, s.dv_t, dqkv, s.gvec,
+            )
+            hidden_point(8 + 2 * j + n)
+
+            def even():
+                rq.guarded(5, j - 2)
+                rq.guarded(3, j - 1)
+                rq.stage(1, j)
+
+            def odd():
+                rq.guarded(6, j - 2)
+                rq.guarded(4, j - 1)
+                rq.stage(2, j)
+
+            pl.when(n == 0)(even)
+            pl.when(n == 1)(odd)
+            return 0
+
+        lax.fori_loop(0, 2, pair, 0)
+        rq.stage_0(j + 1, tn(s.a1[...], dqkv[...]).astype(BF16))
+        for m in range(s.x.shape[0] // BLOCK):
+            at = slice(m * BLOCK, (m + 1) * BLOCK)
+            da1[at, :] += nt(dqkv[at, :], wq[j])
+        return 0
+
+    lax.fori_loop(0, 3, backward, 0)
+    get_x_again.wait()
+    rq.stage(5, 1)
+    rq.stage(3, 2)
+    rq.stage(1, 3)
+    norm_one_back(s.x, s.da2, da1, vecs, s.gvec, s.a1)
+    grad_copy = pltpu.make_async_copy(s.a1, input_grad, s.local.at[1])
+    grad_copy.start()
+    comm.pack_vectors(s.gvec)
+    for step in range(1, 8):
+        comm.vector_copy(1, step).start()
+    rq.stage(6, 1)
+    rq.stage(4, 2)
+    rq.stage(2, 3)
+    outs = comm.outs
+    rows = comm.ins["out"].shape[0]
+    width = s.x.shape[1]
+    x2 = s.x2
+    x2[:rows, :] = rq.total[0].astype(F32)
+    copies = [pltpu.make_async_copy(x2.at[pl.ds(0, rows), :], outs["out"], s.local.at[5])]
+    copies[0].start()
+    for t in range(6):
+        x2[rows + 64 * t : rows + 64 * (t + 1), :] = rd.total[t].astype(F32)
+    copies.append(pltpu.make_async_copy(x2.at[pl.ds(rows, 384), :], outs["down"], s.local.at[6]))
+    copies[1].start()
+    base = rows + 384
+    for group in range(24):
+        owner, t = group // 3, 2 * (group % 3)
+        lanes = slice(64 * owner, 64 * (owner + 1))
+        both = jnp.concatenate([ru.total[t, :, lanes], ru.total[t + 1, :, lanes]], axis=1)
+        at, off = base + rows * (group // 6), 128 * (group % 6)
+        x2[at : at + rows, off : off + 128] = both.astype(F32)
+    for b in range(4):
+        copies.append(
+            pltpu.make_async_copy(
+                x2.at[pl.ds(base + rows * b, rows), :],
+                outs["up"].at[:, pl.ds(width * b, width)],
+                s.local.at[7 + b],
+            )
+        )
+        copies[-1].start()
+    for step in range(1, 8):
+        comm.vector_landed(1, step)
+    share = c["vpack"][here.d]
+    for step in range(1, 8):
+        share = share + c["vin"][step]
+    c["vz"][here.z] = share
+    for step in range(1, 4):
+        comm.vector_copy(2, step).start()
+    rq.stage(5, 2)
+    rq.stage(3, 3)
+
+    def out_qkv(j):
+        for part in range(3):
+            da1[part * rows : (part + 1) * rows, j * BLOCK : (j + 1) * BLOCK] = rq.total[
+                j + 1, :, part * BLOCK : (part + 1) * BLOCK
+            ].astype(F32)
+
+    out_qkv(0)
+    rq.stage(6, 2)
+    rq.stage(4, 3)
+    out_qkv(1)
+    for step in range(1, 4):
+        comm.vector_landed(2, step)
+    vz = c["vz"]
+    outs["vec"][...] = (vz[0] + vz[1]) + (vz[2] + vz[3])
+    gq.drain()
+    gu.drain()
+    gd.drain()
+    for kind, count in ((0, 8), (1, 8), (2, 4)):
+        for step in range(1, count):
+            comm.vector_copy(kind, step).wait_send()
+    rq.stage(5, 3)
+    rq.stage(6, 3)
+    out_qkv(2)
+    for part in range(3):
+        copies.append(
+            pltpu.make_async_copy(
+                da1.at[pl.ds(part * rows, rows), :],
+                outs["qkv"].at[:, pl.ds(width * part, width)],
+                s.local.at[11 + part],
+            )
+        )
+        copies[-1].start()
+    act_copy.wait()
+    grad_copy.wait()
+    for copy in copies:
+        copy.wait()
+
+
+def fused_layer(lengths, task_of, task_tokens, x, grad_out, w_qkv, w_out, w_up, w_down, vec):
+    length, width = x.shape
+    rows = w_out.shape[0]
+    shapes = layer_scratch(length, width)
+    shapes["x"] = pltpu.VMEM((length, width), BF16)
+    shapes["vecs"] = pltpu.VMEM((VEC_ROWS, width), F32)
+    shapes["local"] = pltpu.SemaphoreType.DMA((14,))
+    full = {
+        "q": pltpu.VMEM((4, width, width), BF16),
+        "u": pltpu.VMEM((6, width, TILE), BF16),
+        "d": pltpu.VMEM((6, TILE, width), BF16),
+    }
+    comm_shapes = {
+        "own": pltpu.SemaphoreType.DMA((7,)),
+        "v_send": pltpu.SemaphoreType.DMA((3, 8)),
+        "v_recv": pltpu.SemaphoreType.DMA((3, 8)),
+        "vfull": pltpu.VMEM((8, VEC_ROWS, 128), F32),
+        "vpack": pltpu.VMEM((8, VEC_ROWS, 128), F32),
+        "vin": pltpu.VMEM((8, VEC_ROWS, 128), F32),
+        "vz": pltpu.VMEM((4, VEC_ROWS, 128), F32),
+    }
+    for kind, count in (("q", 4), ("u", 6), ("d", 6)):
+        for name in ("g_send_", "g_recv_", "r_send_", "r_recv_"):
+            comm_shapes[name + kind] = pltpu.SemaphoreType.DMA((8, count))
+    sums = {
+        "q": Reduce.buffers(4, rows, width, 2, 2),
+        "u": Reduce.buffers(6, rows, TILE, 3, 3),
+        "d": Reduce.buffers(6, 64, width, 3, 3),
+    }
+    names, comm_names = tuple(shapes), tuple(comm_shapes)
+    scratch = list(shapes.values()) + list(full.values()) + list(comm_shapes.values())
+    for kind in "qud":
+        scratch += sums[kind]
+
+    def kernel(*refs):
+        refs = list(refs)
+        take = lambda n: [refs.pop(0) for _ in range(n)]
+        lens, of, tokens, hbm_x, hbm_grad = take(5)
+        ins = dict(zip(("qkv", "out", "up", "down", "vec"), take(5)))
+        act, input_grad = take(2)
+        outs = dict(zip(("qkv", "out", "up", "down", "vec"), take(5)))
+        s = Named(names, take(len(names)))
+        g = dict(zip("qud", take(3)))
+        c = dict(zip(comm_names, take(len(comm_names))))
+        for kind in "qud":
+            c["r_" + kind] = take(10)
+        comm = Fused(Place(), ins, outs, g, c)
+        fused_body(comm, lens, of, tokens, hbm_x, hbm_grad, act, input_grad, s.vecs, s)
+
+    smem = pl.BlockSpec(memory_space=pltpu.SMEM)
+    vmem = pl.BlockSpec(memory_space=pltpu.VMEM)
+    hbm = pl.BlockSpec(memory_space=pl.ANY)
+    like = lambda a: jax.ShapeDtypeStruct(a.shape, F32)
+    return pl.pallas_call(
+        kernel,
+        out_shape=(
+            jax.ShapeDtypeStruct(x.shape, BF16), jax.ShapeDtypeStruct(x.shape, BF16),
+            like(w_qkv), like(w_out), like(w_up), like(w_down), like(vec),
+        ),
+        in_specs=[smem] * 3 + [hbm] * 6 + [vmem],
+        out_specs=(hbm,) * 6 + (vmem,),
+        scratch_shapes=scratch,
+        compiler_params=pltpu.CompilerParams(
+            vmem_limit_bytes=63 * 2**20, collective_id=0, has_side_effects=True
+        ),
+        name="layer",
+    )(lengths, task_of, task_tokens, x, grad_out, w_qkv, w_out, w_up, w_down, vec)
+
+
+def fused_shards(
+    tokens, grad_out, lengths, task_of, task_tokens, w_qkv, w_out, w_up, w_down,
+    bias_q, bias_v, bias_out, bias_up, bias_down, gain_one, shift_one, gain_two, shift_two,
+):
+    rows = w_out.shape[0]
+    eight = jnp.stack([bias_q, bias_v, bias_out, bias_down, gain_one, shift_one, gain_two, shift_two])
+    up = bias_up.reshape(6, 64)
+    vec = jnp.concatenate(
+        [
+            jnp.pad(eight, ((0, 0), (0, 128 - rows))),
+            jnp.pad(up, ((0, VEC_ROWS - 8 - 6), (0, 64))),
+        ]
+    ).astype(F32)
+    act, input_grad, gqkv, gout, gup, gdn, gvec = fused_layer(
+        lengths, task_of, task_tokens, tokens[0], grad_out[0], w_qkv, w_out, w_up, w_down, vec
+    )
+    line = lambda n: gvec[n, :rows]
+    return (
+        act[None], input_grad[None], gqkv, gout, gup, gdn, line(BQ), line(BV), line(BO),
+        gvec[UP : UP + 6, :64].reshape(-1), line(BD), line(G1), line(S1), line(G2), line(S2),
+    )
+
+
 def solution(mesh):
     rows = P(("grp", "dp"), None, None)
     each = P(("grp", "dp"))
     matrix, vector = P("dp", None), P("dp")
     in_specs = (rows, rows, each, each, P()) + (matrix,) * 4 + (vector,) * 9
     out_specs = (rows, rows) + (matrix,) * 4 + (vector,) * 9
-    body = plain_body
+    small = mesh.shape["dp"] == 8 and mesh.shape["grp"] == 4
+    body = fused_shards if small else plain_body
     return jax.shard_map(body, mesh=mesh, in_specs=in_specs, out_specs=out_specs, check_vma=False)

time: 613 us -> 208 us (0.34)
  waiting for transfers between devices: 310 us -> 0 us
  blocking collectives: 71 us -> 0 us
  local copies, waits for them, and re-layouts: 69.2 us -> 12.8 us
  Pallas kernels: 136 us -> 192 us
  between operations: 17.3 us -> 1.96 us
  other arithmetic: 8.31 us -> 0.6 us
    reduce_scatter x2 -> x0, waiting for transfers between devices: 96.1 us -> none  [plain_body(): shares = lax.psum_scatter(grads, 'dp', scatter_dimension=0, tiled=True)]
    unnamed x11 -> x0, waiting for transfers between devices: 92.1 us -> none
    all_gather x4 -> x0, waiting for transfers between devices: 72.8 us -> none  [plain_body(): gather = lambda a: lax.all_gather(a, 'dp', axis=0, tiled=True)]
    pallas_call x1, Pallas kernels: 136 us -> 192 us  [fused_layer(): pl.pallas_call(kernel, out_shape=(jax.ShapeDtypeStruct(x.shape, BF16), ja...]
    unnamed x2 -> x0, blocking collectives: 49.9 us -> none
    psum x1 -> x0, waiting for transfers between devices: 48.8 us -> none  [plain_body(): summed = jax.tree.map(lambda a: a.astype(F32), lax.psum(shares, 'grp'))]
    unnamed x39 -> x16, local copies, waits for them, and re-layouts: 29.9 us -> 8.38 us
    psum x1 -> x0, blocking collectives: 13.2 us -> none  [plain_body(): summed = jax.tree.map(lambda a: a.astype(F32), lax.psum(shares, 'grp'))]
  transfers between devices with their start and end apart: 9 -> 0, of which waited for: 8 -> 0; matrix products, arithmetic and copies ran while one was open for 10% -> 0% of each run, Pallas kernels for 0% -> 0%
where the time goes in v2:
time: 208 us
  Pallas kernels  192 us (92%)
  local copies, waits for them, and re-layouts  12.8 us (6%)
    pallas_call x1, Pallas kernels, fused_layer(): pl.pallas_call(kernel, out_shape=(jax.ShapeDtypeStruct(x.shape, BF16), ja...  192 us
    unnamed x16, local copies, waits for them, and re-layouts  8.38 us

profile of v2, /device:TPU:0, one launch (start us, length us, event | category | flops | bytes accessed | tf_op | source)
XLA Modules:
  0.0 207.8 jit_solution(6527730371444636948)
XLA Ops:
  0.6 0.8 reshape.36
  1.4 0.8 stack.35
  2.2 0.6 fusion.3.refs_9_
  4.1 192.4 %layer.1 = (bf16[1024,768]{1,0:T(8,128)(2,1)}, bf16[1024,768]{1,0:T(8,128)(2,1)}, f32[96,2304]{1,0:T(8,128)}, f32[96,768]{1,0:T(8,128)}, f32[96,3072]{1,0:T(8,12...) custom-call(s32[1]{0:T(128)S(6)} %copy.39.refs_0_, s32[1]{0:T(128)S(6)} %copy.40.refs_1_, s32[16]{0:T(128)} %refs_2_.1, ...), custom_call_target="tpu_custom_call" | custom-call | tf_op jit(solution)/shard_map/layer/pallas_call | solution.py:1094
  196.5 1.5 slice_bitcast_fusion
  198.0 0.7 slice.30
  198.7 0.7 reshape.37
  199.4 0.0 copy-start
  199.4 2.8 %copy.41 = bf16[1,1024,768]{2,1,0:T(8,128)(2,1)} copy(bf16[1,1024,768]{2,1,0:T(8,128)(2,1)} %bitcast.29) | data formatting | bytes 3145728
  202.1 0.0 copy-done
  202.1 0.0 copy-start.3
  202.1 1.1 copy.42
  203.3 0.6 copy-done.3
  203.9 0.0 copy-start.4
  203.9 0.0 copy-start.2
  203.9 0.9 copy.43
  204.8 0.2 copy-done.4
  205.0 0.0 copy-start.1
  205.0 0.7 copy.44
  205.7 0.0 copy-done.2
  205.7 1.0 copy.45
  206.7 0.0 copy-done.1
  206.7 1.0 copy.46
Async XLA Ops:
  199.4 2.8 %copy-start = (bf16[1024,768]{1,0:T(8,128)(2,1)S(1)}, bf16[1024,768]{1,0:T(8,128)(2,1)}, u32[]{:S(2)}) copy-start(bf16[1024,768]{1,0:T(8,128)(2,1)} %get-tuple-element.23) | copy-start | bytes 4718596
  202.1 1.7 copy-start.3
  203.9 1.1 copy-start.4
  203.9 1.8 copy-start.2
  205.0 1.7 copy-start.1

commit v3 on v2

--- a/solution.py
+++ b/solution.py
@@ -490,6 +490,8 @@
         self.d_y = d + 4 - 8 * y
         self.d_diag = self.d_x + 4 - 8 * y
         self.chip_x, self.chip_y, self.chip_diag = self.d_x // 2, self.d_y // 2, self.d_diag // 2
+        self.odd = lax.rem(z, 2)
+        self.on_z = (z + 1 - 2 * self.odd, d)
         self.on_core, self.on_x, self.on_y = ((z, e) for e in (self.d_core, self.d_x, self.d_y))
         self.outer = (z == 0) | (z == 3)
         self.inner = (z == 1) | (z == 2)
@@ -511,59 +513,84 @@
         self.here, self.full, self.sems = here, full, sems
         self.count, rows, _ = full.shape
         self.rows = rows // 8
-
-    def block(self, i, owner, half=None):
-        rows = self.rows if half is None else self.rows // 2
-        start = owner * self.rows + (0 if half is None else half * rows)
-        return self.full.at[i, pl.ds(pl.multiple_of(start, 16), rows), :]
+        self.once = (self.rows - 32) // 2
+        self.span = self.rows - self.once
+
+    def block(self, i, owner, start=0, rows=None):
+        rows = self.rows if rows is None else rows
+        at = pl.ds(pl.multiple_of(owner * self.rows + start, 16), rows)
+        return self.full.at[i, at, :]
+
+    def crossing(self, i, owner):
+        return self.block(i, owner, self.here.odd * self.once, self.span)
+
+    def half(self, i, owner, n):
+        start = self.here.odd * self.once + 32 * n
+        return self.block(i, owner, start, 32 if n == 0 else self.span - 32)
+
+    def shared(self, i, owner, odd):
+        return self.block(i, owner, odd * (self.rows - self.once), self.once)
 
     def copy(self, i, n):
         p = self.here
-        owner, half, device = (
-            (p.d, None, p.on_x),
-            (p.d, None, p.on_y),
-            (p.d, None, p.on_core),
-            (p.d_x, None, p.on_core),
-            (p.d_x, 0, p.on_y),
-            (p.d_y, None, p.on_core),
-            (p.d_y, 1, p.on_x),
-            (p.d_diag, None, p.on_core),
-        )[n]
-        part = self.block(i, owner, half)
+        part, device = (
+            lambda: (self.crossing(i, p.d), p.on_x),
+            lambda: (self.crossing(i, p.d), p.on_y),
+            lambda: (self.block(i, p.d), p.on_core),
+            lambda: (self.block(i, p.d_x), p.on_core),
+            lambda: (self.half(i, p.d_x, 0), p.on_y),
+            lambda: (self.block(i, p.d_y), p.on_core),
+            lambda: (self.half(i, p.d_y, 1), p.on_x),
+            lambda: (self.block(i, p.d_diag), p.on_core),
+            lambda: (self.shared(i, p.d_x, p.odd), p.on_z),
+            lambda: (self.shared(i, p.d_y, p.odd), p.on_z),
+            lambda: (self.shared(i, p.d_diag, p.odd), p.on_z),
+        )[n]()
         return remote(part, part, self.sems, (n, i), device)
 
     def landed(self, i, n):
         p = self.here
         flip = 1 - 2 * p.core
-        owner, half = (
-            (p.d_x, None),
-            (p.d_y, None),
-            (p.d_core, None),
-            (p.d_x + flip, None),
-            (p.d_diag, 0),
-            (p.d_y + flip, None),
-            (p.d_diag, 1),
-            (p.d_diag + flip, None),
-        )[n]
-        part = self.block(i, owner, half)
+        part = (
+            lambda: self.crossing(i, p.d_x),
+            lambda: self.crossing(i, p.d_y),
+            lambda: self.block(i, p.d_core),
+            lambda: self.block(i, p.d_x + flip),
+            lambda: self.half(i, p.d_diag, 0),
+            lambda: self.block(i, p.d_y + flip),
+            lambda: self.half(i, p.d_diag, 1),
+            lambda: self.block(i, p.d_diag + flip),
+            lambda: self.shared(i, p.d_x, 1 - p.odd),
+            lambda: self.shared(i, p.d_y, 1 - p.odd),
+            lambda: self.shared(i, p.d_diag, 1 - p.odd),
+        )[n]()
         remote(part, part, self.sems, (n, i), p.on_core).wait_recv()
 
+    def begin(self, i, *numbers):
+        for n in numbers:
+            self.copy(i, n).start()
+
     def start(self, i):
-        for n in (0, 1, 2):
-            self.copy(i, n).start()
+        self.begin(i, 0, 1, 2)
 
     def relay(self, i):
         self.landed(i, 0)
-        self.copy(i, 4).start()
-        self.copy(i, 3).start()
+        self.begin(i, 4, 8)
         self.landed(i, 1)
-        self.copy(i, 6).start()
-        self.copy(i, 5).start()
+        self.begin(i, 6, 9)
 
     def diag(self, i):
         self.landed(i, 4)
         self.landed(i, 6)
-        self.copy(i, 7).start()
+        self.begin(i, 10)
+
+    def hand(self, i):
+        self.landed(i, 8)
+        self.begin(i, 3)
+        self.landed(i, 9)
+        self.begin(i, 5)
+        self.landed(i, 10)
+        self.begin(i, 7)
 
     def need(self, i):
         for n in (2, 3, 5, 7):
@@ -571,7 +598,7 @@
 
     def drain(self):
         def step(i, _):
-            for n in range(8):
+            for n in range(11):
                 self.copy(i, n).wait_send()
             return 0
 
@@ -594,13 +621,13 @@
          self.run, self.from_outer, self.from_mid, self.total) = bufs
         self.count, self.rows, self.columns = self.total.shape
         self.slots, self.run_slots = self.sums.shape[0] - 1, self.run.shape[0]
-        self.outer_slots = self.from_outer.shape[0]
+        self.half_slots, self.side_slots = self.half_x.shape[0], self.from_x.shape[0]
 
     @staticmethod
-    def buffers(count, rows, columns, slots, run_slots):
+    def buffers(count, rows, columns, slots, half_slots, run_slots):
         piece = (rows, columns)
         shapes = [(slots + 1, 4) + piece, (2, 4) + piece]
-        shapes += [(2, rows // 2, columns)] * 2 + [(2,) + piece] * 2
+        shapes += [(half_slots, rows // 2, columns)] * 2 + [(run_slots,) + piece] * 2
         shapes += [(run_slots,) + piece, (run_slots,) + piece, (2,) + piece, (count,) + piece]
         return [pltpu.VMEM(shape, BF16) for shape in shapes]
 
@@ -610,14 +637,15 @@
     def copy(self, i, n):
         p, two, half = self.here, lax.rem(i, 2), self.rows // 2
         own = self.mine(i)
-        run = self.run.at[lax.rem(i, self.run_slots)]
+        at = lax.rem(i, self.run_slots)
+        run, half_at = self.run.at[at], lax.rem(i, self.half_slots)
         src, dst, device = (
             lambda: (self.sums.at[0], self.from_core.at[two], p.on_core),
-            lambda: (self.sums.at[own, p.chip_diag, :half], self.half_x.at[two], p.on_x),
-            lambda: (self.sums.at[own, p.chip_diag, half:], self.half_y.at[two], p.on_y),
-            lambda: (self.sums.at[own, p.chip_x], self.from_x.at[two], p.on_x),
-            lambda: (self.sums.at[own, p.chip_y], self.from_y.at[two], p.on_y),
-            lambda: (run, self.from_outer.at[lax.rem(i, self.outer_slots)], p.to_inner),
+            lambda: (self.sums.at[own, p.chip_diag, :half], self.half_x.at[half_at], p.on_x),
+            lambda: (self.sums.at[own, p.chip_diag, half:], self.half_y.at[half_at], p.on_y),
+            lambda: (self.sums.at[own, p.chip_x], self.from_x.at[at], p.on_x),
+            lambda: (self.sums.at[own, p.chip_y], self.from_y.at[at], p.on_y),
+            lambda: (run, self.from_outer.at[at], p.to_inner),
             lambda: (run, self.from_mid.at[two], p.to_mid),
             lambda: (self.total.at[i], self.total.at[i], p.to_outer),
         )[n]()
@@ -643,21 +671,20 @@
                 self.copy(i, 2).start()
 
     def stage_2(self, i):
-        p, own, two, half = self.here, self.mine(i), lax.rem(i, 2), self.rows // 2
+        p, own, half = self.here, self.mine(i), self.rows // 2
+        at = lax.rem(i, self.half_slots)
         self.copy(i, 1).wait_recv()
-        self.sums[own, p.chip_y, :half] = added(self.sums[own, p.chip_y, :half], self.half_x[two])
+        self.copy(i, 2).wait_recv()
+        self.sums[own, p.chip_y, :half] = added(self.sums[own, p.chip_y, :half], self.half_x[at])
         self.copy(i, 4).start()
-        self.copy(i, 2).wait_recv()
-        self.sums[own, p.chip_x, half:] = added(self.sums[own, p.chip_x, half:], self.half_y[two])
+        self.sums[own, p.chip_x, half:] = added(self.sums[own, p.chip_x, half:], self.half_y[at])
         self.copy(i, 3).start()
 
     def stage_3(self, i):
-        p, own, two = self.here, self.mine(i), lax.rem(i, 2)
+        p, own, at = self.here, self.mine(i), lax.rem(i, self.run_slots)
         self.copy(i, 3).wait_recv()
         self.copy(i, 4).wait_recv()
-        self.run[lax.rem(i, self.run_slots)] = added(
-            self.sums[own, p.chip], self.from_x[two], self.from_y[two]
-        )
+        self.run[at] = added(self.sums[own, p.chip], self.from_x[at], self.from_y[at])
         for n in (1, 2, 3, 4):
             self.copy(i, n).wait_send()
         pl.when(p.outer)(lambda: self.copy(i, 5).start())
@@ -666,7 +693,7 @@
         def work():
             self.copy(i, 5).wait_recv()
             at = lax.rem(i, self.run_slots)
-            self.run[at] = added(self.run[at], self.from_outer[lax.rem(i, self.outer_slots)])
+            self.run[at] = added(self.run[at], self.from_outer[at])
             self.copy(i, 6).start()
 
         pl.when(self.here.inner)(work)
@@ -695,6 +722,10 @@
         getattr(self, "stage_%d" % s)(i)
 
     def guarded(self, s, i):
+        if isinstance(i, int):
+            if 0 <= i < self.count:
+                self.stage(s, i)
+            return
         pl.when((i >= 0) & (i < self.count))(lambda: self.stage(s, i))
 
 
@@ -708,6 +739,35 @@
             kind: Reduce(here, c["r_" + kind], (c["r_send_" + kind], c["r_recv_" + kind]))
             for kind in "qud"
         }
+
+    def gather_step(self, name, item):
+        def tile():
+            for kind in "ud":
+                getattr(self.gather[kind], name)(item - 4)
+
+        def chunk():
+            getattr(self.gather["q"], name)(item)
+
+        if isinstance(item, int):
+            if 0 <= item < 4:
+                chunk()
+            elif 4 <= item < 10:
+                tile()
+        else:
+            pl.when((item >= 0) & (item < 4))(chunk)
+            pl.when((item >= 4) & (item < 10))(tile)
+
+    def gather_point(self, k):
+        if not isinstance(k, int) or k >= 3:
+            self.gather_step("hand", k - 2)
+        self.gather_step("relay", k)
+        self.gather_step("start", k + 2)
+        self.gather_step("diag", k - 1)
+
+    def hidden_point(self, p):
+        for stage, lag in ((6, 7), (5, 6), (4, 5), (3, 4), (1, 1), (2, 2)):
+            for kind in "ud":
+                self.reduce[kind].guarded(stage, p - lag)
 
     def greet(self):
         p, barrier = self.here, pltpu.get_barrier_semaphore()
@@ -828,9 +888,8 @@
         for copy in own[j]:
             copy.wait()
         gq.start(j)
-    for copy in ups:
+    for copy in own[2]:
         copy.wait()
-    comm.place_up(s.o_t)
     own_vec.wait()
     for step in range(1, 8):
         comm.vector_landed(0, step)
@@ -838,83 +897,58 @@
     get_x.wait()
     norm_one_phase(s.x, vecs, s.a1, s.x2)
     get_grad.start()
-    gq.relay(0)
-    for copy in own[2] + own[3] + own[4]:
+    comm.gather_point(0)
+    for copy in ups:
         copy.wait()
-    gq.diag(0)
-
-    def hidden_start(t):
-        gu.start(t)
-        gd.start(t)
-
-    def hidden_relay(t):
-        gu.relay(t)
-        gd.relay(t)
-
-    def hidden_diag(t):
-        gu.diag(t)
-        gd.diag(t)
+    comm.place_up(s.o_t)
+    for copy in own[3] + own[4]:
+        copy.wait()
+    comm.gather_point(1)
+    get_grad.wait()
+    branch_phase(s.x, length_s, weight_s, s.g_f, s.gvec)
+    gq.hand(0)
 
     def forward(j, _):
-        pl.when(j < 2)(lambda: gq.start(j + 2))
-        pl.when(j == 2)(lambda: hidden_start(0))
         gq.need(j)
         qkv_phase(j, s.a1, wq, vecs, s.k, s.v, s.q_t, s.k_t, s.v_t)
-        gq.relay(j + 1)
+        comm.gather_step("relay", 2 * j + 2)
+        comm.gather_step("start", 2 * j + 4)
+        comm.gather_step("diag", 2 * j + 1)
+        pl.when(j > 0)(lambda: comm.gather_step("hand", 2 * j))
 
         def pair(n, _):
             attend_pair(2 * j + n, length_s, s.k, s.q_t, s.v_t, s.o_t, s.lse)
-            pl.when(n == 0)(lambda: gq.diag(j + 1))
+            pl.when(n == 0)(lambda: comm.gather_point(2 * j + 3))
             return 0
 
         return lax.fori_loop(0, 2, pair, 0)
 
     lax.fori_loop(0, 3, forward, 0)
-    hidden_start(1)
-    hidden_relay(0)
-    get_grad.wait()
-    branch_phase(s.x, length_s, weight_s, s.g_f, s.gvec)
     gq.need(3)
     norm_two_phase(s.o_t, wout, vecs, s.x2, s.a2, s.out_acc)
-    hidden_diag(0)
+    comm.gather_point(8)
     hr, gu_tile = s.work.at[:, :TILE], s.work.at[:, TILE:]
 
     def hidden(t, _):
-        pl.when(t < 4)(lambda: hidden_start(t + 2))
         gu.need(t)
         gd.need(t)
         hidden_tile(t, s.a2, s.g_f, wup, wdn, vecs, s.out_acc, s.da2, hr, gu_tile, s.gvec)
-        pl.when(t < 5)(lambda: hidden_relay(t + 1))
-        for stage in range(6, 0, -1):
-            ru.guarded(stage, t - stage)
-            rd.guarded(stage, t - stage)
+        comm.gather_point(9 + t)
+        comm.hidden_point(t)
         ru.stage_0(t, tn(s.a2[...], gu_tile[...]).astype(BF16))
         rd.stage_0(t, tn(hr[...], s.g_f[...]).astype(BF16))
-        pl.when(t < 5)(lambda: hidden_diag(t + 1))
         return 0
 
     lax.fori_loop(0, 6, hidden, 0)
-
-    def hidden_point(step):
-        for stage in range(6, 0, -1):
-            item = step - stage
-            if isinstance(step, int):
-                if 0 <= item < 6:
-                    ru.stage(stage, item)
-                    rd.stage(stage, item)
-            else:
-                ru.guarded(stage, item)
-                rd.guarded(stage, item)
 
     norm_two_back(s.x, length_s, weight_s, s.x2, s.da2, vecs, s.a2, s.gvec, s.out_acc, s.g_f)
     get_x_again.start()
     act_copy = pltpu.make_async_copy(s.g_f, act, s.local.at[0])
     act_copy.start()
-    hidden_point(6)
+    comm.hidden_point(6)
     rq.stage_0(0, nn(s.o_t[...], s.a2[...]).astype(BF16))
     g_o_t = s.v_t
     attended_back(wout, s.a2, s.o_t, g_o_t, s.delta)
-    hidden_point(7)
     da1 = s.out_acc
     da1[...] = jnp.zeros_like(da1)
     dqkv = s.work.at[:, : 3 * BLOCK]
@@ -925,16 +959,16 @@
                 2 * j + n, s.k, s.v, s.q_t, s.k_t, g_o_t, s.lse, s.delta,
                 s.dk_t, s.dv_t, dqkv, s.gvec,
             )
-            hidden_point(8 + 2 * j + n)
+            comm.hidden_point(7 + 2 * j + n)
 
             def even():
+                rq.guarded(6, j - 3)
+                rq.guarded(4, j - 2)
+                rq.stage(1, j)
+
+            def odd():
                 rq.guarded(5, j - 2)
                 rq.guarded(3, j - 1)
-                rq.stage(1, j)
-
-            def odd():
-                rq.guarded(6, j - 2)
-                rq.guarded(4, j - 1)
                 rq.stage(2, j)
 
             pl.when(n == 0)(even)
@@ -950,8 +984,8 @@
 
     lax.fori_loop(0, 3, backward, 0)
     get_x_again.wait()
-    rq.stage(5, 1)
-    rq.stage(3, 2)
+    rq.stage(6, 0)
+    rq.stage(4, 1)
     rq.stage(1, 3)
     norm_one_back(s.x, s.da2, da1, vecs, s.gvec, s.a1)
     grad_copy = pltpu.make_async_copy(s.a1, input_grad, s.local.at[1])
@@ -959,8 +993,8 @@
     comm.pack_vectors(s.gvec)
     for step in range(1, 8):
         comm.vector_copy(1, step).start()
-    rq.stage(6, 1)
-    rq.stage(4, 2)
+    rq.stage(5, 1)
+    rq.stage(3, 2)
     rq.stage(2, 3)
     outs = comm.outs
     rows = comm.ins["out"].shape[0]
@@ -997,7 +1031,8 @@
     c["vz"][here.z] = share
     for step in range(1, 4):
         comm.vector_copy(2, step).start()
-    rq.stage(5, 2)
+    rq.stage(6, 1)
+    rq.stage(4, 2)
     rq.stage(3, 3)
 
     def out_qkv(j):
@@ -1007,8 +1042,9 @@
             ].astype(F32)
 
     out_qkv(0)
+    rq.stage(5, 2)
+    rq.stage(4, 3)
     rq.stage(6, 2)
-    rq.stage(4, 3)
     out_qkv(1)
     for step in range(1, 4):
         comm.vector_landed(2, step)
@@ -1060,12 +1096,14 @@
         "vz": pltpu.VMEM((4, VEC_ROWS, 128), F32),
     }
     for kind, count in (("q", 4), ("u", 6), ("d", 6)):
-        for name in ("g_send_", "g_recv_", "r_send_", "r_recv_"):
+        for name in ("g_send_", "g_recv_"):
+            comm_shapes[name + kind] = pltpu.SemaphoreType.DMA((11, count))
+        for name in ("r_send_", "r_recv_"):
             comm_shapes[name + kind] = pltpu.SemaphoreType.DMA((8, count))
     sums = {
-        "q": Reduce.buffers(4, rows, width, 2, 2),
-        "u": Reduce.buffers(6, rows, TILE, 3, 3),
-        "d": Reduce.buffers(6, 64, width, 3, 3),
+        "q": Reduce.buffers(4, rows, width, 2, 2, 2),
+        "u": Reduce.buffers(6, rows, TILE, 4, 4, 3),
+        "d": Reduce.buffers(6, 64, width, 4, 4, 3),
     }
     names, comm_names = tuple(shapes), tuple(comm_shapes)
     scratch = list(shapes.values()) + list(full.values()) + list(comm_shapes.values())

time: 208 us -> 188 us (0.904)
  Pallas kernels: 192 us -> 173 us
    pallas_call x1, Pallas kernels: 192 us -> 173 us  [fused_layer(): pl.pallas_call(kernel, out_shape=(jax.ShapeDtypeStruct(x.shape, BF16), ja...]
where the time goes in v3:
time: 188 us
  Pallas kernels  173 us (92%)
  local copies, waits for them, and re-layouts  12.8 us (7%)
  between operations  1.96 us (1%)
    pallas_call x1, Pallas kernels, fused_layer(): pl.pallas_call(kernel, out_shape=(jax.ShapeDtypeStruct(x.shape, BF16), ja...  173 us
    unnamed x16, local copies, waits for them, and re-layouts  8.38 us

profile of v3, /device:TPU:0, one launch (start us, length us, event | category | flops | bytes accessed | tf_op | source)
XLA Modules:
  0.0 188.0 jit_solution(15060326141885108841)
XLA Ops:
  0.6 0.8 reshape.36
  1.4 0.8 stack.35
  2.2 0.6 fusion.3.refs_9_
  4.1 172.7 %layer.1 = (bf16[1024,768]{1,0:T(8,128)(2,1)}, bf16[1024,768]{1,0:T(8,128)(2,1)}, f32[96,2304]{1,0:T(8,128)}, f32[96,768]{1,0:T(8,128)}, f32[96,3072]{1,0:T(8,12...) custom-call(s32[1]{0:T(128)S(6)} %copy.39.refs_0_, s32[1]{0:T(128)S(6)} %copy.40.refs_1_, s32[16]{0:T(128)} %refs_2_.1, ...), custom_call_target="tpu_custom_call" | custom-call | tf_op jit(solution)/shard_map/layer/pallas_call | solution.py:1132
  176.8 1.5 slice_bitcast_fusion
  178.3 0.7 slice.30
  179.0 0.7 reshape.37
  179.7 0.0 copy-start
  179.7 2.8 %copy.41 = bf16[1,1024,768]{2,1,0:T(8,128)(2,1)} copy(bf16[1,1024,768]{2,1,0:T(8,128)(2,1)} %bitcast.29) | data formatting | bytes 3145728
  182.4 0.0 copy-done
  182.4 0.0 copy-start.3
  182.4 1.1 copy.42
  183.6 0.6 copy-done.3
  184.2 0.0 copy-start.4
  184.2 0.0 copy-start.2
  184.2 0.9 copy.43
  185.1 0.2 copy-done.4
  185.3 0.0 copy-start.1
  185.3 0.7 copy.44
  186.0 0.0 copy-done.2
  186.0 1.0 copy.45
  187.0 0.0 copy-done.1
  187.0 1.0 copy.46
Async XLA Ops:
  179.7 2.8 %copy-start = (bf16[1024,768]{1,0:T(8,128)(2,1)S(1)}, bf16[1024,768]{1,0:T(8,128)(2,1)}, u32[]{:S(2)}) copy-start(bf16[1024,768]{1,0:T(8,128)(2,1)} %get-tuple-element.23) | copy-start | bytes 4718596
  182.4 1.7 copy-start.3
  184.2 1.1 copy-start.4
  184.2 1.8 copy-start.2
  185.3 1.7 copy-start.1
